TPU v7x, 128 devices: a whole 4x4x4 slice. The times are simulated.
128 devices in a mesh: row: 16 (over z, y), col: 8 (over x, core).
Axes of the slice: x: 4, y: 4, z: 4, core: 2. Of those that a mesh axis runs over, the one named last changes fastest.
Arguments:
- profile_representation: bfloat16 [256, 768, 256], P('col', 'row'), may hold values from -6 to 6
- couple_embedding: bfloat16 [768, 768, 128], P('row', 'col'), may hold values from -6 to 6
- loss_sensitivity_pair: bfloat16 [768, 768, 128], P('row', 'col'), may hold values from -6 to 6
- former_mapping_weights: bfloat16 [256, 32], replicated, may hold values from -0.375 to 0.375
- latter_mapping_weights: bfloat16 [256, 32], replicated, may hold values from -0.375 to 0.375
- tensor_mixing_weights: bfloat16 [1024, 128], replicated, may hold values from -3 to 3
- expand_silu_matrix: bfloat16 [128, 512], replicated, may hold values from -0.5 to 0.5
- shrink_silu_matrix: bfloat16 [512, 128], replicated, may hold values from -0.25 to 0.25
Outputs:
- pairwise_output: bfloat16 [768, 768, 128], P(('row', 'col'))
- pairwise_gradient: bfloat16 [768, 768, 128], P('row', 'col')
- profile_slope_field: bfloat16 [256, 768, 256], P('col', 'row')
All inputs are finite; a program needn't handle non-finite values.
Results may differ from a plain program's by a relative error of at most 0.023.
Values may be sent and summed in bfloat16 or wider, within the bound.
A program may use at most 128 MiB of HBM per device.

v0:
```python
import math

import jax
import jax.numpy as jnp
from jax import lax
from jax.sharding import PartitionSpec as P

epsilon = 1e-05


def perform_rescaling(values):
    center = values - jnp.mean(values, axis=-1, keepdims=True)
    inverse_deviation = lax.rsqrt(jnp.mean(center * center, axis=-1, keepdims=True) + epsilon)
    return (center * inverse_deviation, inverse_deviation)


def rescaling_reverse_pass(incoming_gradient, centered_normed, inverse_deviation):
    outer_mean_gradient = jnp.mean(incoming_gradient, axis=-1, keepdims=True)
    outer_mean_projected = jnp.mean(incoming_gradient * centered_normed, axis=-1, keepdims=True)
    return (
        incoming_gradient - outer_mean_gradient - centered_normed * outer_mean_projected
    ) * inverse_deviation


def on_device(
    profile_representation,
    couple_embedding,
    loss_sensitivity_pair,
    former_mapping_weights,
    latter_mapping_weights,
    tensor_mixing_weights,
    expand_silu_matrix,
    shrink_silu_matrix,
):
    piece_relative_tally, piece_peptide_size, profile_channel_size = profile_representation.shape
    rows, cols, pair_width = couple_embedding.shape
    proj_width = former_mapping_weights.shape[1]
    col_count = lax.axis_size("col")
    seq_total = piece_relative_tally * col_count
    multiplier = 1.0 / seq_total
    whitened_profile_values, profile_unit_scaler = perform_rescaling(
        profile_representation.astype(jnp.float32)
    )
    profile_rescaled = whitened_profile_values.astype(jnp.bfloat16).reshape(
        -1, profile_channel_size
    )
    former_mapped = jnp.dot(
        profile_rescaled, former_mapping_weights, preferred_element_type=jnp.float32
    ).astype(jnp.bfloat16)
    former_mapped = former_mapped.reshape(piece_relative_tally, piece_peptide_size, proj_width)
    latter_mapped = jnp.dot(
        profile_rescaled, latter_mapping_weights, preferred_element_type=jnp.float32
    ).astype(jnp.bfloat16)
    latter_mapped = latter_mapped.reshape(piece_relative_tally, piece_peptide_size, proj_width)
    left_all = lax.all_gather(former_mapped, "col", axis=0, tiled=True)
    right_wide = lax.all_gather(latter_mapped, "row", axis=1, tiled=True)
    right_all = lax.all_to_all(right_wide, "col", split_axis=1, concat_axis=0, tiled=True)
    block = math.gcd(rows, 16)
    count = rows // block

    def step(carry, index):
        start = index * block
        pair_rows = lax.dynamic_slice_in_dim(couple_embedding, start, block, 0)
        cot_rows = lax.dynamic_slice_in_dim(loss_sensitivity_pair, start, block, 0)
        left_rows = lax.dynamic_slice_in_dim(left_all, start, block, 1)
        outer = (
            jnp.einsum("sip,sjq->ijpq", left_rows, right_all, preferred_element_type=jnp.float32)
            * multiplier
        )
        outer = outer.astype(jnp.bfloat16).reshape(block * cols, proj_width * proj_width)
        update = jnp.dot(outer, tensor_mixing_weights, preferred_element_type=jnp.float32)
        mid = (pair_rows.reshape(block * cols, pair_width).astype(jnp.float32) + update).astype(
            jnp.bfloat16
        )
        transition_hidden = mid.astype(jnp.float32)
        pairwise_centered_normed, pairwise_inverse_deviation = perform_rescaling(transition_hidden)
        activation_input = jnp.dot(
            pairwise_centered_normed.astype(jnp.bfloat16),
            expand_silu_matrix,
            preferred_element_type=jnp.float32,
        )
        hidden = jax.nn.silu(activation_input).astype(jnp.bfloat16)
        out_rows = (
            transition_hidden
            + jnp.dot(hidden, shrink_silu_matrix, preferred_element_type=jnp.float32)
        ).astype(jnp.bfloat16)
        cotangent_flat = cot_rows.reshape(block * cols, pair_width)
        hidden_grad = jnp.dot(
            cotangent_flat, shrink_silu_matrix.T, preferred_element_type=jnp.float32
        )
        sigma = jax.nn.sigmoid(activation_input)
        pre_grad = (hidden_grad * sigma * (1.0 + activation_input * (1.0 - sigma))).astype(
            jnp.bfloat16
        )
        normed_gradient = jnp.dot(
            pre_grad, expand_silu_matrix.T, preferred_element_type=jnp.float32
        )
        gradient_rows = (
            cotangent_flat.astype(jnp.float32)
            + rescaling_reverse_pass(
                normed_gradient, pairwise_centered_normed, pairwise_inverse_deviation
            )
        ).astype(jnp.bfloat16)
        outer_grad = jnp.dot(
            gradient_rows, tensor_mixing_weights.T, preferred_element_type=jnp.float32
        ).astype(jnp.bfloat16)
        outer_grad = outer_grad.reshape(block, cols, proj_width, proj_width)
        left_term = (
            jnp.einsum("ijpq,sjq->sip", outer_grad, right_all, preferred_element_type=jnp.float32)
            * multiplier
        )
        right_term = (
            jnp.einsum("ijpq,sip->sjq", outer_grad, left_rows, preferred_element_type=jnp.float32)
            * multiplier
        )
        outs = (
            out_rows.reshape(block, cols, pair_width),
            gradient_rows.reshape(block, cols, pair_width),
            left_term,
        )
        return (carry + right_term, outs)

    initial_accumulator = jnp.zeros((seq_total, cols, proj_width), jnp.float32)
    latter_mapped_slope, (out_blocks, grad_blocks, former_pieces) = lax.scan(
        step, initial_accumulator, jnp.arange(count, dtype=jnp.int32)
    )
    pairwise_output = lax.all_to_all(
        out_blocks.reshape(rows, cols, pair_width), "col", split_axis=0, concat_axis=1, tiled=True
    )
    pairwise_gradient = grad_blocks.reshape(rows, cols, pair_width)
    left_part = jnp.transpose(former_pieces, (1, 0, 2, 3)).reshape(seq_total, rows, proj_width)
    former_mapped_slope = lax.psum_scatter(
        left_part.astype(jnp.bfloat16), "col", scatter_dimension=0, tiled=True
    ).astype(jnp.float32)
    right_moved = lax.all_to_all(
        latter_mapped_slope.astype(jnp.bfloat16), "col", split_axis=0, concat_axis=1, tiled=True
    ).astype(latter_mapped_slope.dtype)
    right_own = lax.psum_scatter(
        right_moved.astype(jnp.bfloat16), "row", scatter_dimension=1, tiled=True
    ).astype(jnp.float32)
    rescaled_profile = jnp.dot(
        former_mapped_slope.reshape(-1, proj_width),
        former_mapping_weights.astype(jnp.float32).T,
        precision=lax.Precision.HIGHEST,
    )
    rescaled_profile = rescaled_profile + jnp.dot(
        right_own.reshape(-1, proj_width),
        latter_mapping_weights.astype(jnp.float32).T,
        precision=lax.Precision.HIGHEST,
    )
    profile_slope_field = rescaling_reverse_pass(
        rescaled_profile.reshape(piece_relative_tally, piece_peptide_size, profile_channel_size),
        whitened_profile_values,
        profile_unit_scaler,
    ).astype(jnp.bfloat16)
    return (pairwise_output, pairwise_gradient, profile_slope_field)


def solution(mesh):
    return jax.shard_map(
        on_device,
        mesh=mesh,
        in_specs=(
            P("col", "row", None),
            P("row", "col", None),
            P("row", "col", None),
            P(),
            P(),
            P(),
            P(),
            P(),
        ),
        out_specs=(P(("row", "col"), None, None), P("row", "col", None), P("col", "row", None)),
        check_vma=False,
    )
```

profile of v0, /device:TPU:7, one launch (start us, length us, event | category | flops | bytes accessed | tf_op | source)
XLA Modules:
  0.0 448.8 jit_solution(14821658811711204953)
XLA Ops:
  7.2 1.5 convert_reduce_fusion
  8.7 1.6 fusion.46
  11.6 1.4 copy.103
  13.1 63.9 %all-gather.2.cloned.1.call-done = bf16[32,768,32]{2,0,1:T(8,128)(2,1)} async-done(((bf16[32,48,32]{2,0,1:T(8,128)(2,1)}), bf16[32,768,32]{2,0,1:T(8,128)(2,1)}) %all-gather.2.cloned.1.call-update) | async-done | bytes 1572880 | tf_op jit(solution)/shard_map/all_gather | solution.py:56
  77.0 9.5 %reshape.115 = bf16[8,2,49152]{2,1,0:T(2,128)(2,1)} reshape(bf16[768,32,32]{2,1,0:T(8,128)(2,1)} %bitcast.161) | data formatting | bytes 3145728
  86.5 5.2 %all-to-all-start = ((bf16[8,2,49152]{2,1,0:T(2,128)(2,1)}), bf16[8,2,49152]{2,1,0:T(2,128)(2,1)}, u32[]{:S(2)}, u32[]{:S(2)}) async-start(bf16[8,2,49152]{2,1,0:T(2,128)(2,1)} %reshape.115), calls=%async_computation | async-start | bytes 3145728 | tf_op jit(solution)/shard_map/all_to_all | solution.py:57
  92.5 29.5 %all_gather.6 = bf16[256,48,32]{1,2,0:T(8,128)(2,1)S(1)} all-gather(bf16[32,48,32]{1,2,0:T(8,128)(2,1)S(1)} %copy.102), channel_id=1, replica_groups=mesh['row'=16,'col'=8] {'col'}, dimensions={0}, use_global_device_ids=true | all-gather | bytes 884736 | tf_op jit(solution)/shard_map/all_gather | solution.py:55
  122.0 3.3 copy.106
  125.3 7.9 %reshape.116 = bf16[768,32,32]{2,1,0:T(8,128)(2,1)} reshape(bf16[8,2,49152]{2,1,0:T(2,128)(2,1)} %all-to-all-done) | data formatting | bytes 3145728
  133.2 7.5 %copy.105 = bf16[8,32,96,32]{2,3,1,0:T(8,128)(2,1)S(1)} copy(bf16[8,32,96,32]{3,1,2,0:T(8,128)(2,1)} %bitcast.152) | data formatting | bytes 3145728 | tf_op jit(solution)/shard_map/all_to_all | solution.py:57
  140.7 2.7 copy.107
  143.9 151.5 %while.17 = (s32[]{:T(128)}, f32[256,96,32]{0,1,2:T(8,128)}, bf16[3,16,96,128]{3,2,1,0:T(8,128)(2,1)}, bf16[3,16,96,128]{3,2,1,0:T(8,128)(2,1)}, bf16[3,256,16,3...) while((s32[]{:T(128)}, f32[256,96,32]{0,1,2:T(8,128)}, ...), condition=%wide.region_7.8_spmd.clone, body=%wide.region_2.7_spmd.clone.sunk | while | flops 4050191872 | bytes 132251064 | solution.py:124
  143.9 1.3 dynamic_slice.36
  145.9 2.8 fusion.108
  148.7 4.6 %copy.145 = bf16[16,96,32,32]{1,0,3,2:T(8,128)(2,1)} copy(bf16[16,96,32,32]{1,2,3,0:T(8,128)(2,1)S(1)} %fusion.108) | data formatting | bytes 6291456 | tf_op jit(solution)/shard_map/while/body/eval_jaxpr/convert_element_type | solution.py:70
  153.3 6.8 %reshape.119 = bf16[1536,1024]{0,1:T(8,128)(2,1)S(1)} reshape(bf16[16,96,32,32]{1,0,3,2:T(8,128)(2,1)} %copy.145) | data formatting | bytes 6291456 | tf_op jit(solution)/shard_map/while/body/eval_jaxpr/reshape | solution.py:70
  160.1 1.0 constant_dynamic-slice_fusion.4
  161.1 1.1 fusion.109
  165.1 1.0 constant_dynamic-slice_fusion.5
  166.1 3.7 fusion.111
  169.8 1.2 add_convert_fusion.2
  173.0 3.0 copy.146
  176.0 7.8 %reshape.120 = bf16[16,96,32,32]{1,0,3,2:T(8,128)(2,1)} reshape(bf16[1536,1024]{0,1:T(8,128)(2,1)} %copy.146) | data formatting | bytes 6291456 | tf_op jit(solution)/shard_map/while/body/eval_jaxpr/reshape | solution.py:107
  183.8 6.1 %fusion.112 = f32[256,96,32]{0,1,2:T(8,128)S(1)} fusion(f32[256,96,32]{0,1,2:T(8,128)S(1)} %copy-done.4, bf16[16,96,32,32]{1,0,3,2:T(8,128)(2,1)} %reshape.120, pred[]{:T(512)S(6)} %compare.3, bf16[256,48,32]{0,2,1:T(8,128)(2,1)} %get-tuple-element.378, s32[]{:T(128)S(6)} %select_n.7), kind=kOutput, calls=%fused_computation.8.clone.1 | convolution fusion | flops 807665664 | bytes 10747909 | tf_op jit(solution)/shard_map/while/body/eval_jaxpr/ijpq,sip->sjq/dot_general | solution.py:113
  189.9 3.7 fusion.114
  194.4 1.3 dynamic_slice.36
  196.3 2.8 fusion.108
  199.1 4.6 %copy.145 = bf16[16,96,32,32]{1,0,3,2:T(8,128)(2,1)} copy(bf16[16,96,32,32]{1,2,3,0:T(8,128)(2,1)S(1)} %fusion.108) | data formatting | bytes 6291456 | tf_op jit(solution)/shard_map/while/body/eval_jaxpr/convert_element_type | solution.py:70
  203.8 6.8 %reshape.119 = bf16[1536,1024]{0,1:T(8,128)(2,1)S(1)} reshape(bf16[16,96,32,32]{1,0,3,2:T(8,128)(2,1)} %copy.145) | data formatting | bytes 6291456 | tf_op jit(solution)/shard_map/while/body/eval_jaxpr/reshape | solution.py:70
  210.6 1.0 constant_dynamic-slice_fusion.4
  211.6 1.1 fusion.109
  216.6 3.7 fusion.111
  220.3 1.2 add_convert_fusion.2
  223.4 3.0 copy.146
  226.5 7.8 %reshape.120 = bf16[16,96,32,32]{1,0,3,2:T(8,128)(2,1)} reshape(bf16[1536,1024]{0,1:T(8,128)(2,1)} %copy.146) | data formatting | bytes 6291456 | tf_op jit(solution)/shard_map/while/body/eval_jaxpr/reshape | solution.py:107
  234.3 6.1 %fusion.112 = f32[256,96,32]{0,1,2:T(8,128)S(1)} fusion(f32[256,96,32]{0,1,2:T(8,128)S(1)} %copy-done.4, bf16[16,96,32,32]{1,0,3,2:T(8,128)(2,1)} %reshape.120, pred[]{:T(512)S(6)} %compare.3, bf16[256,48,32]{0,2,1:T(8,128)(2,1)} %get-tuple-element.378, s32[]{:T(128)S(6)} %select_n.7), kind=kOutput, calls=%fused_computation.8.clone.1 | convolution fusion | flops 807665664 | bytes 10747909 | tf_op jit(solution)/shard_map/while/body/eval_jaxpr/ijpq,sip->sjq/dot_general | solution.py:113
  240.4 3.7 fusion.114
  244.9 1.3 dynamic_slice.36
  246.8 2.8 fusion.108
  249.6 4.6 %copy.145 = bf16[16,96,32,32]{1,0,3,2:T(8,128)(2,1)} copy(bf16[16,96,32,32]{1,2,3,0:T(8,128)(2,1)S(1)} %fusion.108) | data formatting | bytes 6291456 | tf_op jit(solution)/shard_map/while/body/eval_jaxpr/convert_element_type | solution.py:70
  254.3 6.8 %reshape.119 = bf16[1536,1024]{0,1:T(8,128)(2,1)S(1)} reshape(bf16[16,96,32,32]{1,0,3,2:T(8,128)(2,1)} %copy.145) | data formatting | bytes 6291456 | tf_op jit(solution)/shard_map/while/body/eval_jaxpr/reshape | solution.py:70
  261.1 1.0 constant_dynamic-slice_fusion.4
  262.1 1.1 fusion.109
  267.1 3.7 fusion.111
  270.8 1.2 add_convert_fusion.2
  273.9 3.0 copy.146
  276.9 7.8 %reshape.120 = bf16[16,96,32,32]{1,0,3,2:T(8,128)(2,1)} reshape(bf16[1536,1024]{0,1:T(8,128)(2,1)} %copy.146) | data formatting | bytes 6291456 | tf_op jit(solution)/shard_map/while/body/eval_jaxpr/reshape | solution.py:107
  284.7 6.1 %fusion.112 = f32[256,96,32]{0,1,2:T(8,128)S(1)} fusion(f32[256,96,32]{0,1,2:T(8,128)S(1)} %copy-done.4, bf16[16,96,32,32]{1,0,3,2:T(8,128)(2,1)} %reshape.120, pred[]{:T(512)S(6)} %compare.3, bf16[256,48,32]{0,2,1:T(8,128)(2,1)} %get-tuple-element.378, s32[]{:T(128)S(6)} %select_n.7), kind=kOutput, calls=%fused_computation.8.clone.1 | convolution fusion | flops 807665664 | bytes 10747909 | tf_op jit(solution)/shard_map/while/body/eval_jaxpr/ijpq,sip->sjq/dot_general | solution.py:113
  290.9 3.7 fusion.114
  295.4 5.4 %copy.110 = bf16[256,48,32]{1,2,0:T(8,128)(2,1)} copy(bf16[256,48,32]{0,2,1:T(8,128)(2,1)} %bitcast.11) | data formatting | bytes 1572864 | tf_op jit(solution)/shard_map/convert_element_type | solution.py:133
  300.9 2.8 copy.138
  303.7 4.0 copy.113
  307.7 37.1 %all_to_all.54 = bf16[256,96,32]{1,2,0:T(8,128)(2,1)} all-to-all(bf16[256,96,32]{1,2,0:T(8,128)(2,1)S(1)} %copy.113), channel_id=1, replica_groups=mesh['row'=16,'col'=8] {'col'}, dimensions={0} | all-to-all | bytes 3145728 | tf_op jit(solution)/shard_map/all_to_all | solution.py:135
  344.8 7.9 %copy.123 = bf16[32,8,96,32]{3,0,2,1:T(8,128)(2,1)} copy(bf16[32,8,96,32]{2,3,0,1:T(8,128)(2,1)} %bitcast.158) | data formatting | bytes 3145728
  352.7 9.6 %reshape.113 = bf16[768,1024]{1,0:T(8,128)(2,1)} reshape(bf16[768,32,32]{2,1,0:T(8,128)(2,1)} %bitcast.153) | data formatting | bytes 3145728
  362.4 1.2 copy-done.12
  363.6 20.0 %all_to_all.55 = bf16[48,96,128]{2,1,0:T(8,128)(2,1)S(1)} all-to-all(bf16[48,96,128]{2,1,0:T(8,128)(2,1)S(1)} %bitcast.165), channel_id=1, replica_groups=mesh['row'=16,'col'=8] {'col'}, dimensions={0} | all-to-all | bytes 2359296 | tf_op jit(solution)/shard_map/all_to_all | solution.py:127
  383.6 1.1 copy.108
  384.8 1.1 copy.111
  386.1 1.6 fusion.50
  387.7 47.8 %reduce-scatter.7.cloned.1.call-done = bf16[48,1024]{1,0:T(8,128)(2,1)} async-done(((bf16[768,1024]{1,0:T(8,128)(2,1)}), bf16[48,1024]{1,0:T(8,128)(2,1)}) %reduce-scatter.7.cloned.1.call-update) | async-done | bytes 98320
  435.5 1.2 reshape.114
  437.8 2.0 fusion.49
  440.6 1.7 fusion.45
  (127 shorter events, 23.3 us)
Async XLA Ops:
  7.2 3.9 copy-start
  7.2 3.2 copy-start.9
  7.2 69.8 %all-gather.2.cloned.1.call-start = ((), (), s32[]{:S(2)}) async-start(), calls=%async_computation.5 | async-start | bytes 6684672 | tf_op jit(solution)/shard_map/all_gather | solution.py:56
  8.7 2.2 copy-start.13
  10.4 0.6 copy-start.15
  86.5 5.3 %copy-start.17 = (bf16[256,32]{0,1:T(8,128)(2,1)S(1)}, bf16[256,32]{0,1:T(8,128)(2,1)}, u32[]{:S(2)}) copy-start(bf16[256,32]{0,1:T(8,128)(2,1)} %param.13) | copy-start | bytes 49156
  86.5 38.8 %all-to-all-start = ((bf16[8,2,49152]{2,1,0:T(2,128)(2,1)}), bf16[8,2,49152]{2,1,0:T(2,128)(2,1)}, u32[]{:S(2)}, u32[]{:S(2)}) async-start(bf16[8,2,49152]{2,1,0:T(2,128)(2,1)} %reshape.115), calls=%async_computation | async-start | bytes 3145728 | tf_op jit(solution)/shard_map/all_to_all | solution.py:57
  91.7 293.0 %reduce-scatter.5.cloned.1.call-start = ((), (), s32[]{:S(2)}) async-start(), calls=%async_computation.6 | async-start | bytes 2359296 | tf_op jit(solution)/shard_map/reduce_scatter | solution.py:132
  140.7 3.2 copy-start.8
  140.7 3.2 copy-start.11
  162.2 1.2 copy-start.2
  162.8 0.9 copy-start.19
  163.4 1.7 copy-start.7
  166.1 3.7 copy-start.3
  176.0 7.8 %copy-start.4 = (f32[256,96,32]{0,1,2:T(8,128)S(1)}, f32[256,96,32]{0,1,2:T(8,128)}, u32[]{:S(2)}) copy-start(f32[256,96,32]{0,1,2:T(8,128)} %get-tuple-element.356) | copy-start | bytes 9437188 | tf_op jit(solution)/shard_map/while
  183.8 6.1 %copy-start.1 = (bf16[16,96,32,32]{1,0,3,2:T(8,128)(2,1)S(1)}, bf16[16,96,32,32]{1,0,3,2:T(8,128)(2,1)}, u32[]{:S(2)}) copy-start(bf16[16,96,32,32]{1,0,3,2:T(8,128)(2,1)} %reshape.120) | copy-start | bytes 9437188 | tf_op jit(solution)/shard_map/while
  189.9 3.7 copy-start.5
  212.7 1.2 copy-start.2
  213.3 0.9 copy-start.19
  213.9 1.7 copy-start.7
  216.6 3.7 copy-start.3
  226.5 7.8 %copy-start.4 = (f32[256,96,32]{0,1,2:T(8,128)S(1)}, f32[256,96,32]{0,1,2:T(8,128)}, u32[]{:S(2)}) copy-start(f32[256,96,32]{0,1,2:T(8,128)} %get-tuple-element.356) | copy-start | bytes 9437188 | tf_op jit(solution)/shard_map/while
  234.3 6.1 %copy-start.1 = (bf16[16,96,32,32]{1,0,3,2:T(8,128)(2,1)S(1)}, bf16[16,96,32,32]{1,0,3,2:T(8,128)(2,1)}, u32[]{:S(2)}) copy-start(bf16[16,96,32,32]{1,0,3,2:T(8,128)(2,1)} %reshape.120) | copy-start | bytes 9437188 | tf_op jit(solution)/shard_map/while
  240.4 3.7 copy-start.5
  263.2 1.2 copy-start.2
  263.8 0.9 copy-start.19
  264.4 1.7 copy-start.7
  267.1 3.7 copy-start.3
  276.9 7.8 %copy-start.4 = (f32[256,96,32]{0,1,2:T(8,128)S(1)}, f32[256,96,32]{0,1,2:T(8,128)}, u32[]{:S(2)}) copy-start(f32[256,96,32]{0,1,2:T(8,128)} %get-tuple-element.356) | copy-start | bytes 9437188 | tf_op jit(solution)/shard_map/while
  284.7 6.1 %copy-start.1 = (bf16[16,96,32,32]{1,0,3,2:T(8,128)(2,1)S(1)}, bf16[16,96,32,32]{1,0,3,2:T(8,128)(2,1)}, u32[]{:S(2)}) copy-start(bf16[16,96,32,32]{1,0,3,2:T(8,128)(2,1)} %reshape.120) | copy-start | bytes 9437188 | tf_op jit(solution)/shard_map/while
  290.9 3.7 copy-start.5
  295.4 5.5 %copy-start.6 = (f32[256,96,32]{0,1,2:T(8,128)S(1)}, f32[256,96,32]{0,1,2:T(8,128)}, u32[]{:S(2)}) copy-start(f32[256,96,32]{0,1,2:T(8,128)} %get-tuple-element.76) | copy-start | bytes 9437188
  300.8 134.7 %reduce-scatter.7.cloned.1.call-start = ((), (), s32[]{:S(2)}) async-start(), calls=%async_computation.7 | async-start | bytes 1671168
  362.4 1.3 copy-start.12
  383.6 2.5 copy-start.18
  437.7 2.0 copy-start.10
  437.8 2.0 copy-start.14
  437.8 2.0 copy-start.16
Sparse Core Ops, SparseCore 0:
  13.2 63.7 all-gather.1
  301.0 47.1 reduce-scatter.4
  362.5 72.9 reduce-scatter.6
where the time goes:
time: 453 us; the launch traced here: 449 us
  local copies, waits for them, and re-layouts  153 us (34%)
  waiting for transfers between devices  112 us (25%)
  blocking collectives  86.6 us (19%)
  matrix products  64 us (14%)
  between operations  14 us (3%)
  other arithmetic  11.1 us (2%)
  starting transfers between devices  5.33 us (1%)
    all_gather x1, waiting for transfers between devices, on_device(): right_wide = lax.all_gather(latter_mapped, 'row', axis=1, tiled=True)  63.9 us
    unnamed x4, waiting for transfers between devices  47.9 us
    unnamed x33, local copies, waits for them, and re-layouts  43.5 us
    all_to_all x1, blocking collectives, on_device(): lax.all_to_all(latter_mapped_slope.astype(jnp.bfloat16), 'col', split_axi...  37.1 us
    all_gather x1, blocking collectives, on_device(): left_all = lax.all_gather(former_mapped, 'col', axis=0, tiled=True)  29.5 us
    reshape x3, local copies, waits for them, and re-layouts, step(): outer_grad = outer_grad.reshape(block, cols, proj_width, proj_width)  23.4 us
    reshape x3, local copies, waits for them, and re-layouts, step(): outer.astype(jnp.bfloat16).reshape(block * cols, proj_width * proj_width)  20.3 us
    all_to_all x1, blocking collectives, on_device(): lax.all_to_all(out_blocks.reshape(rows, cols, pair_width), 'col', split_a...  20 us
  transfers between devices with their start and end apart: 4, of which 2 were waited for; matrix products, arithmetic and copies ran while one was open for 7% of the time, Pallas kernels for 0%

commit v1 on v0

v1 whole, which is shorter than its diff:
```python
import functools

import jax
import jax.numpy as jnp
from jax import lax
from jax.experimental import pallas as pl
from jax.experimental.pallas import tpu as pltpu
from jax.sharding import PartitionSpec as P

MESH = pl.DeviceIdType.MESH
EPS = 1e-05
F32 = jnp.float32
BF16 = jnp.bfloat16

ROWS, COLS = 16, 8
S, SL = 256, 32
I, J, JP = 48, 96, 128
Q = 32
C, H, CH = 128, 512, 256
SK = S // ROWS
G8 = Q // 4
PK = 3 * G8 * 128
FULL = Q * JP
IB = I // COLS
SLABS = [4 * (k // 3) + k % 3 for k in range(3 * G8)] + [4 * g + 3 for g in range(G8)]


def dot(a, b):
    return jnp.dot(a, b, preferred_element_type=F32)


def dot_nt(a, b):
    return lax.dot_general(a, b, (((1,), (1,)), ((), ())), preferred_element_type=F32)


def eye(n, m=None):
    m = n if m is None else m
    i = lax.broadcasted_iota(jnp.int32, (n, m), 0)
    j = lax.broadcasted_iota(jnp.int32, (n, m), 1)
    return jnp.where(i == j, 1.0, 0.0).astype(BF16)


def lanes(shape):
    return lax.broadcasted_iota(jnp.int32, shape, 1)


def roll(x, shift):
    return pltpu.roll(x, shift, 1)


def pack4(q0, q1, q2, q3):
    ln = lanes(q0.shape)
    return (
        jnp.where(ln < 96, q0, roll(q3, 96)),
        jnp.where(ln < 96, q1, roll(q3, 64)),
        jnp.where(ln < 96, q2, roll(q3, 32)),
    )


def unpack_fourth(t0, t1, t2):
    ln = lanes(t0.shape)
    return jnp.where(ln < 32, roll(t0, 32), jnp.where(ln < 64, roll(t1, 64), roll(t2, 96)))


def kernel(
    x_ref, pair_ref, loss_ref, f_ref, g_ref, w_ref, e_ref, s_ref,
    out_ref, grad_ref, slope_ref,
    xhat, rstd, proj, tq, lall, lt, rhop, rin, rm, xs, ogs, obuf,
    wf32, wf, wt, et, st, lgs, lgt, lgin, rgp, rgin, rh, rhin, hg,
    hop_s, hop_r, lga_s, lga_r, rga_s, rga_r, a2a_s, a2a_r, lrs_s, lrs_r, rrs_s, rrs_r, hop2_s, hop2_r,
):
    r = lax.axis_index("row")
    c = lax.axis_index("col")
    half = lax.rem(r, 2)
    across = lax.div(r, 2)

    barrier = pltpu.get_barrier_semaphore()

    def greet_row(d, _):
        pl.semaphore_signal(barrier, inc=1, device_id=(lax.rem(r + d, ROWS), c), device_id_type=MESH)
        return 0

    def greet_col(d, _):
        pl.semaphore_signal(barrier, inc=1, device_id=(r, lax.rem(c + d, COLS)), device_id_type=MESH)
        return 0

    lax.fori_loop(1, ROWS, greet_row, 0)
    lax.fori_loop(1, COLS, greet_col, 0)
    own = [jnp.logical_and(across == c, half == t) for t in range(2)]
    for t in range(2):
        @pl.when(jnp.logical_not(own[t]))
        def _():
            pl.semaphore_signal(barrier, inc=1, device_id=(2 * c + t, across), device_id_type=MESH)

    iden = eye(C)
    ln128 = lanes((SL, 128))
    tile4 = jnp.where(
        lax.rem(lax.broadcasted_iota(jnp.int32, (Q, 128), 1), Q)
        == lax.broadcasted_iota(jnp.int32, (Q, 128), 0), 1.0, 0.0).astype(BF16)
    f4 = dot(f_ref[...], tile4).astype(BF16)
    gt = dot_nt(eye(Q), g_ref[...]).astype(BF16)
    tq[...] = jnp.zeros_like(tq)

    def project(b, _):
        rows = 4 * I
        at = pl.multiple_of(b * rows, rows)
        x = x_ref[pl.ds(b * 4, 4)].reshape(rows, CH).astype(F32)
        center = x - jnp.mean(x, axis=-1, keepdims=True)
        inv = lax.rsqrt(jnp.mean(center * center, axis=-1, keepdims=True) + EPS)
        xn = center * inv
        xhat[pl.ds(at, rows), :] = xn
        rstd[pl.ds(at, rows), :] = inv
        xb = xn.astype(BF16)
        proj[pl.ds(at, rows), :] = dot(xb, f4)
        for k in range(4):
            to = pl.multiple_of((b * 4 + k) * Q, Q)
            tq[pl.ds(to, Q), 0:I] = dot_nt(gt, xb[k * I:(k + 1) * I])
        return 0

    lax.fori_loop(0, SL // 4, project, 0)

    mine = pl.ds(pl.multiple_of(c * SL, SL), SL)
    for qp in range(Q // 2):
        even = tq[pl.ds(2 * qp, SL, stride=Q), :]
        odd = tq[pl.ds(2 * qp + 1, SL, stride=Q), :]
        rhop[qp] = jnp.where(ln128 < 64, even, roll(odd, 64)).astype(BF16)
    for g in range(I // 4):
        parts = [proj[pl.ds(4 * g + a, SL, stride=I), :] for a in range(4)]
        tile = jnp.where(ln128 < 32, parts[0], jnp.where(ln128 < 64, parts[1],
                         jnp.where(ln128 < 96, parts[2], parts[3])))
        lall[mine, g * 128:(g + 1) * 128] = tile.astype(BF16)

    pl.semaphore_wait(barrier, ROWS + COLS - (across == c).astype(jnp.int32))

    def hop_remote(src, dst, t, ss, rs):
        return pltpu.make_async_remote_copy(
            src_ref=src, dst_ref=dst, send_sem=ss.at[t], recv_sem=rs,
            device_id=(2 * c + t, across), device_id_type=MESH)

    def hop_start(src, dst, t, ss, rs):
        @pl.when(own[t])
        def _():
            pltpu.make_async_copy(src, dst, rs).start()

        @pl.when(jnp.logical_not(own[t]))
        def _():
            hop_remote(src, dst, t, ss, rs).start()

    def hop_wait(src, dst, t, ss, rs):
        @pl.when(own[t])
        def _():
            pltpu.make_async_copy(src, dst, rs).wait()

        @pl.when(jnp.logical_not(own[t]))
        def _():
            hop_remote(src, dst, t, ss, rs).wait_recv()

    def hop_sent(src, dst, t, ss, rs):
        @pl.when(jnp.logical_not(own[t]))
        def _():
            hop_remote(src, dst, t, ss, rs).wait_send()

    for t in range(2):
        hop_start(rhop.at[:, pl.ds(SK * t, SK), :], rin.at[half], t, hop_s, hop_r.at[half])

    def l_copy(d):
        return pltpu.make_async_remote_copy(
            src_ref=lall.at[mine], dst_ref=lall.at[mine], send_sem=lga_s.at[d], recv_sem=lga_r.at[d],
            device_id=(r, lax.rem(c + d, COLS)), device_id_type=MESH)

    def l_start(d, _):
        l_copy(d).start()
        return 0

    lax.fori_loop(1, COLS, l_start, 0)

    for t in range(2):
        hop_wait(rhop.at[:, pl.ds(SK * t, SK), :], rin.at[t], t, hop_s, hop_r.at[t])

    ln16 = lanes((SK, 128))
    here = pl.ds(pl.multiple_of(r * SK, SK), SK)
    for g in range(G8):
        tiles = []
        for k in range(2):
            a = rin[0, 2 * g + k].astype(F32)
            b = rin[1, 2 * g + k].astype(F32)
            tiles.append(jnp.where(ln16 < 48, a, roll(b, 48)))
            tiles.append(jnp.where(ln16 < 48, roll(a, 64), roll(b, 112)))
        for k, tile in enumerate(pack4(*tiles)):
            rm[here, (3 * g + k) * 128:(3 * g + k + 1) * 128] = tile.astype(BF16)

    def r_copy(d):
        return pltpu.make_async_remote_copy(
            src_ref=rm.at[here, pl.ds(0, PK)], dst_ref=rm.at[here, pl.ds(0, PK)],
            send_sem=rga_s.at[d], recv_sem=rga_r.at[d],
            device_id=(lax.rem(r + d, ROWS), c), device_id_type=MESH)

    def r_start(d, _):
        r_copy(d).start()
        return 0

    lax.fori_loop(1, ROWS, r_start, 0)

    wf32[...] = w_ref[...].astype(F32)
    for k, q in enumerate(SLABS):
        wf[k * Q:(k + 1) * Q, :] = wf32[pl.ds(q, Q, stride=Q), :].astype(BF16)
    wt[...] = dot_nt(iden, wf[...]).astype(BF16)
    st[...] = dot_nt(iden, s_ref[...]).astype(BF16)
    et[...] = dot_nt(eye(H), e_ref[...]).astype(BF16)

    def l_wait(d, _):
        l_copy(d).wait_recv()
        return 0

    lax.fori_loop(1, COLS, l_wait, 0)
    e256 = eye(S)
    for k in range(I * Q // S):
        lt[k * S:(k + 1) * S, :] = dot_nt(e256, lall[:, k * S:(k + 1) * S]).astype(BF16)

    def r_wait(d, _):
        r_copy(d).wait_recv()
        return 0

    lax.fori_loop(1, ROWS, r_wait, 0)
    for g in range(G8):
        t0, t1, t2 = [rm[:, (3 * g + k) * 128:(3 * g + k + 1) * 128].astype(F32) for k in range(3)]
        rm[:, (3 * G8 + g) * 128:(3 * G8 + g + 1) * 128] = unpack_fourth(t0, t1, t2).astype(BF16)

    def a2a_copy(t):
        to = lax.rem(c + 1 + t, COLS)
        return pltpu.make_async_remote_copy(
            src_ref=obuf.at[pl.ds(to * IB, IB)], dst_ref=out_ref.at[:, pl.ds(pl.multiple_of(c * J, J), J), :],
            send_sem=a2a_s.at[t], recv_sem=a2a_r.at[t], device_id=(r, to), device_id_type=MESH)

    def own_copy():
        return pltpu.make_async_copy(
            obuf.at[pl.ds(c * IB, IB)], out_ref.at[:, pl.ds(pl.multiple_of(c * J, J), J), :],
            a2a_s.at[COLS - 1])

    pad = jnp.zeros((JP - J, C), BF16)
    scale = 1.0 / S

    def block(t, _):
        ib = lax.rem(c + 1 + t, COLS)
        ip = pl.ds(pl.multiple_of(ib * (IB * Q), IB * Q), IB * Q)
        ltb = lt[ip, :]
        for ch in range(8):
            d = dot(ltb, rm[:, ch * 512:(ch + 1) * 512]).astype(BF16)
            for k in range(4):
                slab = ch * 4 + k
                for i in range(IB):
                    xs[slab * Q:(slab + 1) * Q, i * JP:(i + 1) * JP] = d[i * Q:(i + 1) * Q, k * 128:(k + 1) * 128]
        for half_block in range(IB // 2):
            i0 = ib * IB + 2 * half_block
            ls = slice(half_block * 256, half_block * 256 + 256)
            upd = dot(wt[...], xs[:, ls]) * scale
            pr = jnp.concatenate([pair_ref[i0], pad, pair_ref[i0 + 1], pad], axis=0)
            lo = jnp.concatenate([loss_ref[i0], pad, loss_ref[i0 + 1], pad], axis=0)
            mid = (dot_nt(iden, pr) + upd).astype(BF16).astype(F32)
            center = mid - jnp.mean(mid, axis=0, keepdims=True)
            inv = lax.rsqrt(jnp.mean(center * center, axis=0, keepdims=True) + EPS)
            xn = center * inv
            pre = dot(et[...], xn.astype(BF16))
            hgr = dot_nt(s_ref[...], lo)
            sg = 0.5 * jnp.tanh(0.5 * pre) + 0.5
            hid = pre * sg
            pgr = (hgr * (sg + hid * (1.0 - sg))).astype(BF16)
            outb = (mid + dot(st[...], hid.astype(BF16))).astype(BF16)
            hatg = dot(e_ref[...], pgr)
            m1 = jnp.mean(hatg, axis=0, keepdims=True)
            m2 = jnp.mean(hatg * xn, axis=0, keepdims=True)
            gb = (dot_nt(iden, lo) + (hatg - m1 - xn * m2) * inv).astype(BF16)
            for i in range(2):
                sl = slice(i * JP, (i + 1) * JP)
                obuf[i0 + i] = dot_nt(iden[0:J], outb[:, sl]).astype(BF16)
                grad_ref[i0 + i] = dot_nt(iden[0:J], gb[:, sl]).astype(BF16)
            og = dot(wf[...], gb).astype(BF16)
            for i in range(2):
                to = pl.ds(pl.multiple_of((i0 + i) * Q, Q), Q)
                for k in range(Q):
                    ogs[to, k * 128:(k + 1) * 128] = og[k * Q:(k + 1) * Q, i * JP:(i + 1) * JP]

        @pl.when(t < COLS - 1)
        def _():
            a2a_copy(t).start()

        @pl.when(t == COLS - 1)
        def _():
            own_copy().start()

        lgs[ip, :] = dot_nt(ogs[ip, :], rm[...]).astype(BF16)
        return 0

    lax.fori_loop(0, COLS, block, 0)

    for k in range(I * Q // S):
        lgt[:, k * S:(k + 1) * S] = dot_nt(e256, lgs[k * S:(k + 1) * S, :]).astype(BF16)

    def lrs_copy(d):
        to = lax.rem(c + d, COLS)
        return pltpu.make_async_remote_copy(
            src_ref=lgt.at[pl.ds(pl.multiple_of(to * SL, SL), SL)], dst_ref=lgin.at[d],
            send_sem=lrs_s.at[d], recv_sem=lrs_r.at[d], device_id=(r, to), device_id_type=MESH)

    def lrs_start(d, _):
        lrs_copy(d).start()
        return 0

    lax.fori_loop(1, COLS, lrs_start, 0)

    for g in range(0, G8, 2):
        a = dot(lall[...], ogs[:, 3 * g * 128:(3 * g + 6) * 128])
        b = dot(lall[...], ogs[:, (3 * G8 + g) * 128:(3 * G8 + g + 2) * 128])
        for k in range(2):
            tiles = pack4(*[a[:, (3 * k + m) * 128:(3 * k + m + 1) * 128] for m in range(3)],
                          b[:, k * 128:(k + 1) * 128])
            for m in range(3):
                at = (3 * (g + k) + m) * 128
                rgp[:, at:at + 128] = tiles[m].astype(BF16)

    def rrs_copy(d):
        to = lax.rem(r + d, ROWS)
        return pltpu.make_async_remote_copy(
            src_ref=rgp.at[pl.ds(pl.multiple_of(to * SK, SK), SK)], dst_ref=rgin.at[d],
            send_sem=rrs_s.at[d], recv_sem=rrs_r.at[d], device_id=(to, c), device_id_type=MESH)

    def rrs_start(d, _):
        rrs_copy(d).start()
        return 0

    lax.fori_loop(1, ROWS, rrs_start, 0)

    def lrs_wait(d, _):
        lrs_copy(d).wait_recv()
        return 0

    lax.fori_loop(1, COLS, lrs_wait, 0)
    f4t = dot_nt(tile4.T, f_ref[...]).astype(BF16)
    g4t = dot_nt(tile4.T, g_ref[...]).astype(BF16)
    zero = jnp.zeros((SL, 128), F32)
    for g in range(I // 4):
        sl = slice(g * 128, (g + 1) * 128)
        tot = lgt[mine, sl].astype(F32)
        for d in range(1, COLS):
            tot = tot + lgin[d, :, sl].astype(F32)
        rows4 = jnp.concatenate(
            [jnp.where(jnp.logical_and(ln128 >= 32 * a, ln128 < 32 * a + 32), tot, zero) for a in range(4)], axis=0)
        res = dot(rows4.astype(BF16), f4t)
        for a in range(4):
            for k in range(2):
                hg[k, pl.ds(4 * g + a, SL, stride=I), :] = res[a * SL:(a + 1) * SL, k * 128:(k + 1) * 128]

    def rrs_wait(d, _):
        rrs_copy(d).wait_recv()
        return 0

    lax.fori_loop(1, ROWS, rrs_wait, 0)
    for g in range(G8):
        tiles = []
        for m in range(3):
            sl = slice((3 * g + m) * 128, (3 * g + m + 1) * 128)
            tot = rgp[here, sl].astype(F32)
            for d in range(1, ROWS):
                tot = tot + rgin[d, :, sl].astype(F32)
            tiles.append(tot)
        tiles.append(unpack_fourth(*tiles))
        for k in range(2):
            even, odd = tiles[2 * k], tiles[2 * k + 1]
            rh[0, 2 * g + k] = jnp.where(ln16 < 64, even, roll(odd, 64)).astype(BF16)
            rh[1, 2 * g + k] = jnp.where(ln16 < 64, roll(even, 80), roll(odd, 16)).astype(BF16)
    for t in range(2):
        hop_start(rh.at[t], rhin.at[half], t, hop2_s, hop2_r.at[half])
    for t in range(2):
        hop_wait(rh.at[t], rhin.at[t], t, hop2_s, hop2_r.at[t])
    for qp in range(Q // 2):
        both = jnp.concatenate([rhin[0, qp], rhin[1, qp]], axis=0).astype(F32)
        tq[pl.ds(2 * qp, SL, stride=Q), :] = both
        tq[pl.ds(2 * qp + 1, SL, stride=Q), :] = roll(both, 64)
    iden_i = eye(I, 128)
    lni = lanes((I, 128))

    def finish(b, _):
        rows = 4 * I
        at = pl.multiple_of(b * rows, rows)
        tj = dot_nt(iden_i, tq[pl.ds(pl.multiple_of(b * 128, 128), 128), :].astype(BF16))
        parts = [jnp.where(jnp.logical_and(lni >= 32 * a, lni < 32 * a + 32), tj, 0.0) for a in range(4)]
        right = dot(jnp.concatenate(parts, axis=0).astype(BF16), g4t)
        left = jnp.concatenate([hg[0, pl.ds(at, rows), :], hg[1, pl.ds(at, rows), :]], axis=1)
        grad = (left + right) * scale
        xn = xhat[pl.ds(at, rows), :]
        m1 = jnp.mean(grad, axis=-1, keepdims=True)
        m2 = jnp.mean(grad * xn, axis=-1, keepdims=True)
        res = (grad - m1 - xn * m2) * rstd[pl.ds(at, rows), :]
        slope_ref[pl.ds(b * 4, 4)] = res.astype(BF16).reshape(4, I, CH)
        return 0

    lax.fori_loop(0, SL // 4, finish, 0)

    def drain_col(d, _):
        l_copy(d).wait_send()
        lrs_copy(d).wait_send()
        a2a_copy(d - 1).wait()
        return 0

    def drain_row(d, _):
        r_copy(d).wait_send()
        rrs_copy(d).wait_send()
        return 0

    lax.fori_loop(1, COLS, drain_col, 0)
    lax.fori_loop(1, ROWS, drain_row, 0)
    own_copy().wait()
    for t in range(2):
        hop_sent(rhop.at[:, pl.ds(SK * t, SK), :], rin.at[half], t, hop_s, hop_r.at[half])
        hop_sent(rh.at[t], rhin.at[half], t, hop2_s, hop2_r.at[half])


def on_device(*args):
    vmem = pl.BlockSpec(memory_space=pltpu.VMEM)
    dma = pltpu.SemaphoreType.DMA
    return pl.pallas_call(
        kernel,
        out_shape=(
            jax.ShapeDtypeStruct((IB, J * COLS, C), BF16),
            jax.ShapeDtypeStruct((I, J, C), BF16),
            jax.ShapeDtypeStruct((SL, I, CH), BF16),
        ),
        in_specs=[vmem] * 8,
        out_specs=(pl.BlockSpec(memory_space=pl.ANY), vmem, vmem),
        scratch_shapes=[
            pltpu.VMEM((SL * I, CH), F32),
            pltpu.VMEM((SL * I, 1), F32),
            pltpu.VMEM((SL * I, 128), F32),
            pltpu.VMEM((SL * Q, 128), F32),
            pltpu.VMEM((S, I * Q), BF16),
            pltpu.VMEM((I * Q, S), BF16),
            pltpu.VMEM((Q // 2, SL, 128), BF16),
            pltpu.VMEM((2, Q // 2, SK, 128), BF16),
            pltpu.VMEM((S, FULL), BF16),
            pltpu.VMEM((Q * Q, IB * JP), BF16),
            pltpu.VMEM((I * Q, FULL), BF16),
            pltpu.VMEM((I, J, C), BF16),
            pltpu.VMEM((Q * Q, C), F32),
            pltpu.VMEM((Q * Q, C), BF16),
            pltpu.VMEM((C, Q * Q), BF16),
            pltpu.VMEM((H, C), BF16),
            pltpu.VMEM((C, H), BF16),
            pltpu.VMEM((I * Q, S), BF16),
            pltpu.VMEM((S, I * Q), BF16),
            pltpu.VMEM((COLS, SL, I * Q), BF16),
            pltpu.VMEM((S, PK), BF16),
            pltpu.VMEM((ROWS, SK, PK), BF16),
            pltpu.VMEM((2, Q // 2, SK, 128), BF16),
            pltpu.VMEM((2, Q // 2, SK, 128), BF16),
            pltpu.VMEM((2, SL * I, 128), F32),
            dma((2,)), dma((2,)),
            dma((COLS,)), dma((COLS,)),
            dma((ROWS,)), dma((ROWS,)),
            dma((COLS,)), dma((COLS,)),
            dma((COLS,)), dma((COLS,)),
            dma((ROWS,)), dma((ROWS,)),
            dma((2,)), dma((2,)),
        ],
        compiler_params=pltpu.CompilerParams(
            collective_id=0, has_side_effects=True, vmem_limit_bytes=60 * 1024 * 1024),
        cost_estimate=pl.CostEstimate(flops=16_000_000_000, bytes_accessed=8_000_000, transcendentals=3_000_000),
    )(*args)


def solution(mesh):
    return jax.shard_map(
        on_device,
        mesh=mesh,
        in_specs=(P("col", "row", None), P("row", "col", None), P("row", "col", None), P(), P(), P(), P(), P()),
        out_specs=(P(("row", "col"), None, None), P("row", "col", None), P("col", "row", None)),
        check_vma=False,
    )
```

time: 453 us -> 140 us (0.31)
  the two profiles are of different devices: /device:TPU:7 before, /device:TPU:109 now
where the time goes in v1:
time: 140 us
  Pallas kernels  131 us (94%)
  local copies, waits for them, and re-layouts  7.8 us (6%)
    pallas_call x1, Pallas kernels, on_device(): pl.pallas_call(kernel, out_shape=(jax.ShapeDtypeStruct((IB, J * COLS, C),...  131 us
    unnamed x9, local copies, waits for them, and re-layouts  7.8 us

profile of v1, /device:TPU:109, one launch (start us, length us, event | category | flops | bytes accessed | tf_op | source)
XLA Modules:
  0.0 139.7 jit_solution(1260569893989543560)
XLA Ops:
  0.6 1.5 %copy.11.f_ref = bf16[256,32]{1,0:T(8,128)(2,1)} copy(bf16[256,32]{0,1:T(8,128)(2,1)} %param.11) | data formatting | bytes 32768 | tf_op args[3]
  2.1 1.4 %copy.12.g_ref = bf16[256,32]{1,0:T(8,128)(2,1)} copy(bf16[256,32]{0,1:T(8,128)(2,1)} %param.12) | data formatting | bytes 32768 | tf_op args[4]
  3.5 131.2 %shard_map.103 = (bf16[6,768,128]{2,1,0:T(8,128)(2,1)}, bf16[48,96,128]{2,1,0:T(8,128)(2,1)}, bf16[32,48,256]{2,1,0:T(8,128)(2,1)}) custom-call(bf16[32,48,256]{2,1,0:T(8,128)(2,1)} %x_ref.1, bf16[48,96,128]{2,1,0:T(8,128)(2,1)} %pair_ref.1, bf16[48,96,128]{2,1,0:T(8,128)(2,1)} %loss_ref.1, bf16[256,32]{1,0:T(8,128)(2,1)} %copy.11.f_ref, ...), custom_call_target="tpu_custom_call" | custom-call | flops 16000000000 | bytes 8000000 | tf_op jit(solution)/shard_map/pallas_call | solution.py:421
  134.7 0.0 copy-start
  134.8 2.5 %copy.16 = bf16[6,768,128]{2,1,0:T(8,128)(2,1)} copy(bf16[6,768,128]{2,1,0:T(8,128)(2,1)} %get-tuple-element.6) | data formatting | bytes 2359296
  137.2 0.0 copy-done
  137.2 0.0 copy-start.1
  137.2 1.0 copy.17
  138.2 0.5 copy-done.1
  138.8 0.9 copy.18
Async XLA Ops:
  134.7 2.5 %copy-start = (bf16[48,96,128]{2,1,0:T(8,128)(2,1)S(1)}, bf16[48,96,128]{2,1,0:T(8,128)(2,1)}, u32[]{:S(2)}) copy-start(bf16[48,96,128]{2,1,0:T(8,128)(2,1)} %get-tuple-element.7) | copy-start | bytes 3538948
  137.2 1.6 %copy-start.1 = (bf16[32,48,256]{2,1,0:T(8,128)(2,1)S(1)}, bf16[32,48,256]{2,1,0:T(8,128)(2,1)}, u32[]{:S(2)}) copy-start(bf16[32,48,256]{2,1,0:T(8,128)(2,1)} %get-tuple-element.8) | copy-start | bytes 2359300

commit v2 on v1

--- a/solution.py
+++ b/solution.py
@@ -66,25 +66,32 @@
     x_ref, pair_ref, loss_ref, f_ref, g_ref, w_ref, e_ref, s_ref,
     out_ref, grad_ref, slope_ref,
     xhat, rstd, proj, tq, lall, lt, rhop, rin, rm, xs, ogs, obuf,
-    wf32, wf, wt, et, st, lgs, lgt, lgin, rgp, rgin, rh, rhin, hg,
-    hop_s, hop_r, lga_s, lga_r, rga_s, rga_r, a2a_s, a2a_r, lrs_s, lrs_r, rrs_s, rrs_r, hop2_s, hop2_r,
+    wf32, wf, wt, et, st, lgt, rgp, rh, rhin, hg, ct, lot, hgs, rmt, r_relay, r_main, l_relay, l_main, l_sib,
+    hop_s, hop_r, ag_s, ag_r, sib_s, sib_r, a2a_s, a2a_r, rs_s, rs_r, hop2_s, hop2_r,
 ):
     r = lax.axis_index("row")
     c = lax.axis_index("col")
     half = lax.rem(r, 2)
     across = lax.div(r, 2)
 
+    z, y = lax.div(r, 4), lax.rem(r, 4)
+    x, core = lax.div(c, 2), lax.rem(c, 2)
+
     barrier = pltpu.get_barrier_semaphore()
 
-    def greet_row(d, _):
-        pl.semaphore_signal(barrier, inc=1, device_id=(lax.rem(r + d, ROWS), c), device_id_type=MESH)
-        return 0
+    def at_row(z_, y_):
+        return 4 * lax.rem(z_ + 4, 4) + lax.rem(y_ + 4, 4)
+
+    def at_col(x_):
+        return 2 * lax.rem(x_ + 4, 4) + core
+
+    for row in (at_row(z - 1, y), at_row(z + 1, y), at_row(z, y - 1), at_row(z, y + 1)):
+        pl.semaphore_signal(barrier, inc=1, device_id=(row, c), device_id_type=MESH)
 
     def greet_col(d, _):
         pl.semaphore_signal(barrier, inc=1, device_id=(r, lax.rem(c + d, COLS)), device_id_type=MESH)
         return 0
 
-    lax.fori_loop(1, ROWS, greet_row, 0)
     lax.fori_loop(1, COLS, greet_col, 0)
     own = [jnp.logical_and(across == c, half == t) for t in range(2)]
     for t in range(2):
@@ -95,26 +102,26 @@
     iden = eye(C)
     ln128 = lanes((SL, 128))
     tile4 = jnp.where(
-        lax.rem(lax.broadcasted_iota(jnp.int32, (Q, 128), 1), Q)
-        == lax.broadcasted_iota(jnp.int32, (Q, 128), 0), 1.0, 0.0).astype(BF16)
-    f4 = dot(f_ref[...], tile4).astype(BF16)
-    gt = dot_nt(eye(Q), g_ref[...]).astype(BF16)
+        lax.rem(lax.broadcasted_iota(jnp.int32, (128, Q), 0), Q)
+        == lax.broadcasted_iota(jnp.int32, (128, Q), 1), 1.0, 0.0).astype(BF16)
+    f4t = dot(tile4, f_ref[...]).astype(BF16)
+    g4t = dot(tile4, g_ref[...]).astype(BF16)
     tq[...] = jnp.zeros_like(tq)
 
     def project(b, _):
         rows = 4 * I
         at = pl.multiple_of(b * rows, rows)
-        x = x_ref[pl.ds(b * 4, 4)].reshape(rows, CH).astype(F32)
-        center = x - jnp.mean(x, axis=-1, keepdims=True)
+        xr = x_ref[pl.ds(b * 4, 4)].reshape(rows, CH).astype(F32)
+        center = xr - jnp.mean(xr, axis=-1, keepdims=True)
         inv = lax.rsqrt(jnp.mean(center * center, axis=-1, keepdims=True) + EPS)
         xn = center * inv
         xhat[pl.ds(at, rows), :] = xn
         rstd[pl.ds(at, rows), :] = inv
         xb = xn.astype(BF16)
-        proj[pl.ds(at, rows), :] = dot(xb, f4)
+        proj[pl.ds(at, rows), :] = dot_nt(xb, f4t)
         for k in range(4):
             to = pl.multiple_of((b * 4 + k) * Q, Q)
-            tq[pl.ds(to, Q), 0:I] = dot_nt(gt, xb[k * I:(k + 1) * I])
+            tq[pl.ds(to, Q), 0:I] = dot_nt(g_ref[...], xb[k * I:(k + 1) * I])
         return 0
 
     lax.fori_loop(0, SL // 4, project, 0)
@@ -130,7 +137,7 @@
                          jnp.where(ln128 < 96, parts[2], parts[3])))
         lall[mine, g * 128:(g + 1) * 128] = tile.astype(BF16)
 
-    pl.semaphore_wait(barrier, ROWS + COLS - (across == c).astype(jnp.int32))
+    pl.semaphore_wait(barrier, 4 + COLS - 1 + 2 - (across == c).astype(jnp.int32))
 
     def hop_remote(src, dst, t, ss, rs):
         return pltpu.make_async_remote_copy(
@@ -163,16 +170,25 @@
     for t in range(2):
         hop_start(rhop.at[:, pl.ds(SK * t, SK), :], rin.at[half], t, hop_s, hop_r.at[half])
 
-    def l_copy(d):
-        return pltpu.make_async_remote_copy(
-            src_ref=lall.at[mine], dst_ref=lall.at[mine], send_sem=lga_s.at[d], recv_sem=lga_r.at[d],
-            device_id=(r, lax.rem(c + d, COLS)), device_id_type=MESH)
-
-    def l_start(d, _):
-        l_copy(d).start()
+    wf32[...] = w_ref[...].astype(F32)
+    for k, q in enumerate(SLABS):
+        wf[k * Q:(k + 1) * Q, :] = wf32[pl.ds(q, Q, stride=Q), :].astype(BF16)
+    wt[...] = dot_nt(iden, wf[...]).astype(BF16)
+    st[...] = dot_nt(iden, s_ref[...]).astype(BF16)
+    et[...] = dot_nt(eye(H), e_ref[...]).astype(BF16)
+    pad = jnp.zeros((JP - J, C), BF16)
+
+    def ahead(k, _):
+        to = pl.ds(pl.multiple_of(k * 256, 256), 256)
+        pr = jnp.concatenate([pair_ref[2 * k], pad, pair_ref[2 * k + 1], pad], axis=0)
+        lo = jnp.concatenate([loss_ref[2 * k], pad, loss_ref[2 * k + 1], pad], axis=0)
+        ct[:, to] = dot_nt(iden, pr).astype(BF16)
+        lob = dot_nt(iden, lo).astype(BF16)
+        lot[:, to] = lob
+        hgs[:, to] = dot(s_ref[...], lob).astype(BF16)
         return 0
 
-    lax.fori_loop(1, COLS, l_start, 0)
+    lax.fori_loop(0, 12, ahead, 0)
 
     for t in range(2):
         hop_wait(rhop.at[:, pl.ds(SK * t, SK), :], rin.at[t], t, hop_s, hop_r.at[t])
@@ -189,39 +205,96 @@
         for k, tile in enumerate(pack4(*tiles)):
             rm[here, (3 * g + k) * 128:(3 * g + k + 1) * 128] = tile.astype(BF16)
 
-    def r_copy(d):
+    def send(src, dst, ss, rs, to):
         return pltpu.make_async_remote_copy(
-            src_ref=rm.at[here, pl.ds(0, PK)], dst_ref=rm.at[here, pl.ds(0, PK)],
-            send_sem=rga_s.at[d], recv_sem=rga_r.at[d],
-            device_id=(lax.rem(r + d, ROWS), c), device_id_type=MESH)
-
-    def r_start(d, _):
-        r_copy(d).start()
-        return 0
-
-    lax.fori_loop(1, ROWS, r_start, 0)
-
-    wf32[...] = w_ref[...].astype(F32)
-    for k, q in enumerate(SLABS):
-        wf[k * Q:(k + 1) * Q, :] = wf32[pl.ds(q, Q, stride=Q), :].astype(BF16)
-    wt[...] = dot_nt(iden, wf[...]).astype(BF16)
-    st[...] = dot_nt(iden, s_ref[...]).astype(BF16)
-    et[...] = dot_nt(eye(H), e_ref[...]).astype(BF16)
-
-    def l_wait(d, _):
-        l_copy(d).wait_recv()
-        return 0
-
-    lax.fori_loop(1, COLS, l_wait, 0)
+            src_ref=src, dst_ref=dst, send_sem=ss, recv_sem=rs, device_id=to, device_id_type=MESH)
+
+    def gather_ring(sl, to, g):
+        return [
+            send(sl(0, 0, 2), sl(0, 0, 2), ag_s.at[g, 0], ag_r.at[g, 0], to(1)),
+            send(sl(0, 0, 2), sl(0, 0, 2), ag_s.at[g, 1], ag_r.at[g, 1], to(-1)),
+            send(sl(-1, 0, 1), sl(-1, 0, 1), ag_s.at[g, 2], ag_r.at[g, 2], to(1)),
+            send(sl(1, 1, 1), sl(1, 1, 1), ag_s.at[g, 3], ag_r.at[g, 3], to(-1)),
+        ]
+
+    def scatter_ring(sl, relay, main, to, g):
+        return [
+            send(sl(2, 0, 1), relay.at[0], rs_s.at[g, 0], rs_r.at[g, 0], to(1)),
+            send(sl(2, 1, 1), relay.at[1], rs_s.at[g, 1], rs_r.at[g, 1], to(-1)),
+            send(sl(1, 0, 2), main.at[0], rs_s.at[g, 2], rs_r.at[g, 2], to(1)),
+            send(sl(-1, 0, 2), main.at[1], rs_s.at[g, 3], rs_r.at[g, 3], to(-1)),
+        ]
+
+    def chunk(ref, side, along_z, w):
+        def sl(off, first, count):
+            row = at_row(z + off, y + w) if along_z else at_row(z + w, y + off)
+            return ref.at[pl.ds(pl.multiple_of(row * SK, SK), SK), pl.ds(side * (PK // 2) + first * (PK // 4), count * (PK // 4))]
+        return sl
+
+    def along(along_z):
+        return lambda d: (at_row(z + d, y), c) if along_z else (at_row(z, y + d), c)
+
+    def l_chunk(ref):
+        def sl(off, first, count):
+            return ref.at[pl.ds(pl.multiple_of(at_col(x + off) * SL, SL), SL), pl.ds(first * (I * Q // 2), count * (I * Q // 2))]
+        return sl
+
+    def to_x(d):
+        return (r, at_col(x + d))
+
+    sibling = (r, c + 1 - 2 * core)
+    STEPS = (0, -1, 1, 2)
+    first = [gather_ring(chunk(rm, k, k == 1, 0), along(k == 1), 5 * k) for k in range(2)]
+    second = [[gather_ring(chunk(rm, k, k == 0, w), along(k == 0), 5 * k + 1 + n)
+               for n, w in enumerate(STEPS)] for k in range(2)]
+    l_ring = gather_ring(l_chunk(lall), to_x, 10)
+    l_sibs = [send(l_chunk(lall)(w, 0, 2), l_chunk(lall)(w, 0, 2), sib_s.at[n], sib_r.at[n], sibling)
+              for n, w in enumerate(STEPS)]
+    for k in range(2):
+        first[k][0].start()
+        first[k][1].start()
+    for k in range(2):
+        second[k][0][0].start()
+        second[k][0][1].start()
+    l_ring[0].start()
+    l_ring[1].start()
+    l_sibs[0].start()
+    lax.fori_loop(12, 15, ahead, 0)
+    for m in range(2):
+        for k in range(2):
+            first[k][m].wait_recv()
+            first[k][2 + m].start()
+            second[k][1 + m][0].start()
+            second[k][1 + m][1].start()
+    lax.fori_loop(15, 18, ahead, 0)
+    for k in range(2):
+        first[k][2].wait_recv()
+        first[k][3].wait_recv()
+        second[k][3][0].start()
+        second[k][3][1].start()
+    for m in range(2):
+        l_ring[m].wait_recv()
+        l_ring[2 + m].start()
+        l_sibs[1 + m].start()
+    for n in range(4):
+        for m in range(2):
+            for k in range(2):
+                second[k][n][m].wait_recv()
+                second[k][n][2 + m].start()
+        if n < 2:
+            lax.fori_loop(18 + 3 * n, 21 + 3 * n, ahead, 0)
+    l_ring[2].wait_recv()
+    l_ring[3].wait_recv()
+    l_sibs[3].start()
+    for n in range(4):
+        l_sibs[n].wait_recv()
     e256 = eye(S)
     for k in range(I * Q // S):
         lt[k * S:(k + 1) * S, :] = dot_nt(e256, lall[:, k * S:(k + 1) * S]).astype(BF16)
-
-    def r_wait(d, _):
-        r_copy(d).wait_recv()
-        return 0
-
-    lax.fori_loop(1, ROWS, r_wait, 0)
+    for n in range(4):
+        for k in range(2):
+            second[k][n][2].wait_recv()
+            second[k][n][3].wait_recv()
     for g in range(G8):
         t0, t1, t2 = [rm[:, (3 * g + k) * 128:(3 * g + k + 1) * 128].astype(F32) for k in range(3)]
         rm[:, (3 * G8 + g) * 128:(3 * G8 + g + 1) * 128] = unpack_fourth(t0, t1, t2).astype(BF16)
@@ -237,7 +310,6 @@
             obuf.at[pl.ds(c * IB, IB)], out_ref.at[:, pl.ds(pl.multiple_of(c * J, J), J), :],
             a2a_s.at[COLS - 1])
 
-    pad = jnp.zeros((JP - J, C), BF16)
     scale = 1.0 / S
 
     def block(t, _):
@@ -254,14 +326,13 @@
             i0 = ib * IB + 2 * half_block
             ls = slice(half_block * 256, half_block * 256 + 256)
             upd = dot(wt[...], xs[:, ls]) * scale
-            pr = jnp.concatenate([pair_ref[i0], pad, pair_ref[i0 + 1], pad], axis=0)
-            lo = jnp.concatenate([loss_ref[i0], pad, loss_ref[i0 + 1], pad], axis=0)
-            mid = (dot_nt(iden, pr) + upd).astype(BF16).astype(F32)
+            here_l = pl.ds(pl.multiple_of(i0 * JP, 2 * JP), 2 * JP)
+            mid = (ct[:, here_l].astype(F32) + upd).astype(BF16).astype(F32)
             center = mid - jnp.mean(mid, axis=0, keepdims=True)
             inv = lax.rsqrt(jnp.mean(center * center, axis=0, keepdims=True) + EPS)
             xn = center * inv
             pre = dot(et[...], xn.astype(BF16))
-            hgr = dot_nt(s_ref[...], lo)
+            hgr = hgs[:, here_l].astype(F32)
             sg = 0.5 * jnp.tanh(0.5 * pre) + 0.5
             hid = pre * sg
             pgr = (hgr * (sg + hid * (1.0 - sg))).astype(BF16)
@@ -269,7 +340,7 @@
             hatg = dot(e_ref[...], pgr)
             m1 = jnp.mean(hatg, axis=0, keepdims=True)
             m2 = jnp.mean(hatg * xn, axis=0, keepdims=True)
-            gb = (dot_nt(iden, lo) + (hatg - m1 - xn * m2) * inv).astype(BF16)
+            gb = (lot[:, here_l].astype(F32) + (hatg - m1 - xn * m2) * inv).astype(BF16)
             for i in range(2):
                 sl = slice(i * JP, (i + 1) * JP)
                 obuf[i0 + i] = dot_nt(iden[0:J], outb[:, sl]).astype(BF16)
@@ -288,26 +359,14 @@
         def _():
             own_copy().start()
 
-        lgs[ip, :] = dot_nt(ogs[ip, :], rm[...]).astype(BF16)
         return 0
 
     lax.fori_loop(0, COLS, block, 0)
 
-    for k in range(I * Q // S):
-        lgt[:, k * S:(k + 1) * S] = dot_nt(e256, lgs[k * S:(k + 1) * S, :]).astype(BF16)
-
-    def lrs_copy(d):
-        to = lax.rem(c + d, COLS)
-        return pltpu.make_async_remote_copy(
-            src_ref=lgt.at[pl.ds(pl.multiple_of(to * SL, SL), SL)], dst_ref=lgin.at[d],
-            send_sem=lrs_s.at[d], recv_sem=lrs_r.at[d], device_id=(r, to), device_id_type=MESH)
-
-    def lrs_start(d, _):
-        lrs_copy(d).start()
-        return 0
-
-    lax.fori_loop(1, COLS, lrs_start, 0)
-
+    big = [[scatter_ring(chunk(rgp, k, k == 0, w), r_relay.at[k, n], r_main.at[k, n], along(k == 0), 5 * k + n)
+            for n, w in enumerate(STEPS)] for k in range(2)]
+    small = [scatter_ring(chunk(rgp, k, k == 1, 0), r_relay.at[k, 4], r_main.at[k, 4], along(k == 1), 5 * k + 4)
+             for k in range(2)]
     for g in range(0, G8, 2):
         a = dot(lall[...], ogs[:, 3 * g * 128:(3 * g + 6) * 128])
         b = dot(lall[...], ogs[:, (3 * G8 + g) * 128:(3 * G8 + g + 2) * 128])
@@ -317,59 +376,87 @@
             for m in range(3):
                 at = (3 * (g + k) + m) * 128
                 rgp[:, at:at + 128] = tiles[m].astype(BF16)
-
-    def rrs_copy(d):
-        to = lax.rem(r + d, ROWS)
-        return pltpu.make_async_remote_copy(
-            src_ref=rgp.at[pl.ds(pl.multiple_of(to * SK, SK), SK)], dst_ref=rgin.at[d],
-            send_sem=rrs_s.at[d], recv_sem=rrs_r.at[d], device_id=(to, c), device_id_type=MESH)
-
-    def rrs_start(d, _):
-        rrs_copy(d).start()
-        return 0
-
-    lax.fori_loop(1, ROWS, rrs_start, 0)
-
-    def lrs_wait(d, _):
-        lrs_copy(d).wait_recv()
-        return 0
-
-    lax.fori_loop(1, COLS, lrs_wait, 0)
-    f4t = dot_nt(tile4.T, f_ref[...]).astype(BF16)
-    g4t = dot_nt(tile4.T, g_ref[...]).astype(BF16)
+        if g % 4 == 2:
+            for n in range(4):
+                big[g // 4][n][0].start()
+                big[g // 4][n][1].start()
+
+    def add(dst, *srcs):
+        tot = dst[...].astype(F32)
+        for src in srcs:
+            tot = tot + src[...].astype(F32)
+        dst[...] = tot.astype(BF16)
+
+    def left_grad(k):
+        part = dot(ogs[k * S:(k + 1) * S, :], rmt[...]).astype(BF16)
+        lgt[:, k * S:(k + 1) * S] = dot_nt(e256, part).astype(BF16)
+
+    def relayed(ring, sl, relay):
+        ring[0].wait_recv()
+        add(sl(1, 0, 1), relay.at[0])
+        ring[2].start()
+        ring[1].wait_recv()
+        add(sl(-1, 1, 1), relay.at[1])
+        ring[3].start()
+
+    for ch in range(FULL // S):
+        rmt[ch * S:(ch + 1) * S, :] = dot_nt(e256, rm[:, ch * S:(ch + 1) * S]).astype(BF16)
+    left_grad(0)
+    for n, w in enumerate(STEPS):
+        for k in range(2):
+            relayed(big[k][n], chunk(rgp, k, k == 0, w), r_relay.at[k, n])
+    for k in range(1, I * Q // S):
+        left_grad(k)
+    l_swap = [send(lgt.at[pl.ds(pl.multiple_of((2 * n + 1 - core) * SL, SL), SL)], l_sib.at[n],
+                   sib_s.at[4 + n], sib_r.at[4 + n], sibling) for n in range(4)]
+    for n in range(4):
+        l_swap[n].start()
+    for n, w in reversed(list(enumerate(STEPS))):
+        for k in range(2):
+            big[k][n][2].wait_recv()
+            big[k][n][3].wait_recv()
+            add(chunk(rgp, k, k == 0, w)(0, 0, 2), r_main.at[k, n, 0], r_main.at[k, n, 1])
+    for k in range(2):
+        small[k][0].start()
+        small[k][1].start()
+    for n in range(4):
+        l_swap[n].wait_recv()
+        add(lgt.at[pl.ds(pl.multiple_of((2 * n + core) * SL, SL), SL)], l_sib.at[n])
+    l_back = scatter_ring(l_chunk(lgt), l_relay, l_main, to_x, 10)
+    l_back[0].start()
+    l_back[1].start()
+    for k in range(2):
+        relayed(small[k], chunk(rgp, k, k == 1, 0), r_relay.at[k, 4])
+    relayed(l_back, l_chunk(lgt), l_relay)
+    for k in range(2):
+        small[k][2].wait_recv()
+        small[k][3].wait_recv()
+    for g in range(G8):
+        tiles = []
+        for m in range(3):
+            at = (3 * g + m) * 128
+            k, sl = at // (PK // 2), slice(at % (PK // 2), at % (PK // 2) + 128)
+            tiles.append(rgp[here, at:at + 128].astype(F32) + r_main[k, 4, 0, :, sl].astype(F32)
+                         + r_main[k, 4, 1, :, sl].astype(F32))
+        tiles.append(unpack_fourth(*tiles))
+        for k in range(2):
+            even, odd = tiles[2 * k], tiles[2 * k + 1]
+            rh[0, 2 * g + k] = jnp.where(ln16 < 64, even, roll(odd, 64)).astype(BF16)
+            rh[1, 2 * g + k] = jnp.where(ln16 < 64, roll(even, 80), roll(odd, 16)).astype(BF16)
+    for t in range(2):
+        hop_start(rh.at[t], rhin.at[half], t, hop2_s, hop2_r.at[half])
+    l_back[2].wait_recv()
+    l_back[3].wait_recv()
     zero = jnp.zeros((SL, 128), F32)
     for g in range(I // 4):
         sl = slice(g * 128, (g + 1) * 128)
-        tot = lgt[mine, sl].astype(F32)
-        for d in range(1, COLS):
-            tot = tot + lgin[d, :, sl].astype(F32)
+        tot = lgt[mine, sl].astype(F32) + l_main[0, :, sl].astype(F32) + l_main[1, :, sl].astype(F32)
         rows4 = jnp.concatenate(
             [jnp.where(jnp.logical_and(ln128 >= 32 * a, ln128 < 32 * a + 32), tot, zero) for a in range(4)], axis=0)
         res = dot(rows4.astype(BF16), f4t)
         for a in range(4):
             for k in range(2):
                 hg[k, pl.ds(4 * g + a, SL, stride=I), :] = res[a * SL:(a + 1) * SL, k * 128:(k + 1) * 128]
-
-    def rrs_wait(d, _):
-        rrs_copy(d).wait_recv()
-        return 0
-
-    lax.fori_loop(1, ROWS, rrs_wait, 0)
-    for g in range(G8):
-        tiles = []
-        for m in range(3):
-            sl = slice((3 * g + m) * 128, (3 * g + m + 1) * 128)
-            tot = rgp[here, sl].astype(F32)
-            for d in range(1, ROWS):
-                tot = tot + rgin[d, :, sl].astype(F32)
-            tiles.append(tot)
-        tiles.append(unpack_fourth(*tiles))
-        for k in range(2):
-            even, odd = tiles[2 * k], tiles[2 * k + 1]
-            rh[0, 2 * g + k] = jnp.where(ln16 < 64, even, roll(odd, 64)).astype(BF16)
-            rh[1, 2 * g + k] = jnp.where(ln16 < 64, roll(even, 80), roll(odd, 16)).astype(BF16)
-    for t in range(2):
-        hop_start(rh.at[t], rhin.at[half], t, hop2_s, hop2_r.at[half])
     for t in range(2):
         hop_wait(rh.at[t], rhin.at[t], t, hop2_s, hop2_r.at[t])
     for qp in range(Q // 2):
@@ -396,26 +483,21 @@
 
     lax.fori_loop(0, SL // 4, finish, 0)
 
-    def drain_col(d, _):
-        l_copy(d).wait_send()
-        lrs_copy(d).wait_send()
-        a2a_copy(d - 1).wait()
+    def drain(t, _):
+        a2a_copy(t).wait()
         return 0
 
-    def drain_row(d, _):
-        r_copy(d).wait_send()
-        rrs_copy(d).wait_send()
-        return 0
-
-    lax.fori_loop(1, COLS, drain_col, 0)
-    lax.fori_loop(1, ROWS, drain_row, 0)
+    lax.fori_loop(0, COLS - 1, drain, 0)
+    for ring in first + second[0] + second[1] + big[0] + big[1] + small + [l_ring, l_back, l_sibs, l_swap]:
+        for copy in ring:
+            copy.wait_send()
     own_copy().wait()
     for t in range(2):
         hop_sent(rhop.at[:, pl.ds(SK * t, SK), :], rin.at[half], t, hop_s, hop_r.at[half])
         hop_sent(rh.at[t], rhin.at[half], t, hop2_s, hop2_r.at[half])
 
 
-def on_device(*args):
+def on_device(profile, pair, loss, former, latter, mixing, expand, shrink):
     vmem = pl.BlockSpec(memory_space=pltpu.VMEM)
     dma = pltpu.SemaphoreType.DMA
     return pl.pallas_call(
@@ -445,26 +527,31 @@
             pltpu.VMEM((C, Q * Q), BF16),
             pltpu.VMEM((H, C), BF16),
             pltpu.VMEM((C, H), BF16),
-            pltpu.VMEM((I * Q, S), BF16),
             pltpu.VMEM((S, I * Q), BF16),
-            pltpu.VMEM((COLS, SL, I * Q), BF16),
             pltpu.VMEM((S, PK), BF16),
-            pltpu.VMEM((ROWS, SK, PK), BF16),
             pltpu.VMEM((2, Q // 2, SK, 128), BF16),
             pltpu.VMEM((2, Q // 2, SK, 128), BF16),
             pltpu.VMEM((2, SL * I, 128), F32),
+            pltpu.VMEM((C, I * JP), BF16),
+            pltpu.VMEM((C, I * JP), BF16),
+            pltpu.VMEM((H, I * JP), BF16),
+            pltpu.VMEM((FULL, S), BF16),
+            pltpu.VMEM((2, 5, 2, SK, PK // 4), BF16),
+            pltpu.VMEM((2, 5, 2, SK, PK // 2), BF16),
+            pltpu.VMEM((2, SL, I * Q // 2), BF16),
+            pltpu.VMEM((2, SL, I * Q), BF16),
+            pltpu.VMEM((4, SL, I * Q), BF16),
             dma((2,)), dma((2,)),
+            dma((11, 4)), dma((11, 4)),
+            dma((8,)), dma((8,)),
             dma((COLS,)), dma((COLS,)),
-            dma((ROWS,)), dma((ROWS,)),
-            dma((COLS,)), dma((COLS,)),
-            dma((COLS,)), dma((COLS,)),
-            dma((ROWS,)), dma((ROWS,)),
+            dma((11, 4)), dma((11, 4)),
             dma((2,)), dma((2,)),
         ],
         compiler_params=pltpu.CompilerParams(
             collective_id=0, has_side_effects=True, vmem_limit_bytes=60 * 1024 * 1024),
         cost_estimate=pl.CostEstimate(flops=16_000_000_000, bytes_accessed=8_000_000, transcendentals=3_000_000),
-    )(*args)
+    )(profile, pair, loss, former.T, latter.T, mixing, expand, shrink)
 
 
 def solution(mesh):

time: 140 us -> 108 us (0.77)
  the two profiles are of different devices: /device:TPU:109 before, /device:TPU:7 now
where the time goes in v2:
time: 108 us; the launch traced here: 107 us
  Pallas kernels  101 us (94%)
  local copies, waits for them, and re-layouts  4.9 us (5%)
    pallas_call x1, Pallas kernels, on_device(): pl.pallas_call(kernel, out_shape=(jax.ShapeDtypeStruct((IB, J * COLS, C),...  101 us
    unnamed x7, local copies, waits for them, and re-layouts  4.9 us

profile of v2, /device:TPU:7, one launch (start us, length us, event | category | flops | bytes accessed | tf_op | source)
XLA Modules:
  0.0 106.8 jit_solution(11314815710993042304)
XLA Ops:
  0.6 101.3 %shard_map.103 = (bf16[6,768,128]{2,1,0:T(8,128)(2,1)}, bf16[48,96,128]{2,1,0:T(8,128)(2,1)}, bf16[32,48,256]{2,1,0:T(8,128)(2,1)}) custom-call(bf16[32,48,256]{2,1,0:T(8,128)(2,1)} %x_ref.1, bf16[48,96,128]{2,1,0:T(8,128)(2,1)} %pair_ref.1, bf16[48,96,128]{2,1,0:T(8,128)(2,1)} %loss_ref.1, bf16[32,256]{1,0:T(8,128)(2,1)} %bitcast.2, ...), custom_call_target="tpu_custom_call" | custom-call | flops 16000000000 | bytes 8000000 | tf_op jit(solution)/shard_map/pallas_call | solution.py:503
  101.9 0.0 copy-start
  101.9 2.5 %copy.14 = bf16[6,768,128]{2,1,0:T(8,128)(2,1)} copy(bf16[6,768,128]{2,1,0:T(8,128)(2,1)} %get-tuple-element.6) | data formatting | bytes 2359296
  104.4 0.0 copy-done
  104.4 0.0 copy-start.1
  104.4 1.0 copy.15
  105.4 0.5 copy-done.1
  105.9 0.9 copy.16
Async XLA Ops:
  101.9 2.5 %copy-start = (bf16[48,96,128]{2,1,0:T(8,128)(2,1)S(1)}, bf16[48,96,128]{2,1,0:T(8,128)(2,1)}, u32[]{:S(2)}) copy-start(bf16[48,96,128]{2,1,0:T(8,128)(2,1)} %get-tuple-element.7) | copy-start | bytes 3538948
  104.4 1.6 %copy-start.1 = (bf16[32,48,256]{2,1,0:T(8,128)(2,1)S(1)}, bf16[32,48,256]{2,1,0:T(8,128)(2,1)}, u32[]{:S(2)}) copy-start(bf16[32,48,256]{2,1,0:T(8,128)(2,1)} %get-tuple-element.8) | copy-start | bytes 2359300

commit v3 on v2

--- a/solution.py
+++ b/solution.py
@@ -57,6 +57,16 @@
     )
 
 
+def squeeze(t0, t1, t2, t3):
+    inner = lax.rem(lanes(t0.shape), 64)
+    return [jnp.where(inner < 48, t, roll(t3, 48 - 16 * k)) for k, t in enumerate((t0, t1, t2))]
+
+
+def restore(t0, t1, t2):
+    inner = lax.rem(lanes(t0.shape), 64)
+    return [t0, t1, t2, jnp.where(inner < 16, roll(t0, 80), jnp.where(inner < 32, roll(t1, 96), roll(t2, 112)))]
+
+
 def unpack_fourth(t0, t1, t2):
     ln = lanes(t0.shape)
     return jnp.where(ln < 32, roll(t0, 32), jnp.where(ln < 64, roll(t1, 64), roll(t2, 96)))
@@ -66,7 +76,7 @@
     x_ref, pair_ref, loss_ref, f_ref, g_ref, w_ref, e_ref, s_ref,
     out_ref, grad_ref, slope_ref,
     xhat, rstd, proj, tq, lall, lt, rhop, rin, rm, xs, ogs, obuf,
-    wf32, wf, wt, et, st, lgt, rgp, rh, rhin, hg, ct, lot, hgs, rmt, r_relay, r_main, l_relay, l_main, l_sib,
+    wf32, wf, wt, et, st, lgt, rgp, rh, rhin, hg, ct, lot, hgs, r_relay, r_main, r_small, l_relay, l_main, l_sib,
     hop_s, hop_r, ag_s, ag_r, sib_s, sib_r, a2a_s, a2a_r, rs_s, rs_r, hop2_s, hop2_r,
 ):
     r = lax.axis_index("row")
@@ -85,7 +95,7 @@
     def at_col(x_):
         return 2 * lax.rem(x_ + 4, 4) + core
 
-    for row in (at_row(z - 1, y), at_row(z + 1, y), at_row(z, y - 1), at_row(z, y + 1)):
+    for row in (at_row(z - 1, y), at_row(z + 1, y), at_row(z + 2, y), at_row(z, y - 1), at_row(z, y + 1), at_row(z, y + 2)):
         pl.semaphore_signal(barrier, inc=1, device_id=(row, c), device_id_type=MESH)
 
     def greet_col(d, _):
@@ -127,17 +137,21 @@
     lax.fori_loop(0, SL // 4, project, 0)
 
     mine = pl.ds(pl.multiple_of(c * SL, SL), SL)
-    for qp in range(Q // 2):
-        even = tq[pl.ds(2 * qp, SL, stride=Q), :]
-        odd = tq[pl.ds(2 * qp + 1, SL, stride=Q), :]
-        rhop[qp] = jnp.where(ln128 < 64, even, roll(odd, 64)).astype(BF16)
+    for m in range(4):
+        pairs = []
+        for qp in range(4 * m, 4 * m + 4):
+            even = tq[pl.ds(2 * qp, SL, stride=Q), :]
+            odd = tq[pl.ds(2 * qp + 1, SL, stride=Q), :]
+            pairs.append(jnp.where(ln128 < 64, even, roll(odd, 64)))
+        for k, tile in enumerate(squeeze(*pairs)):
+            rhop[3 * m + k] = tile.astype(BF16)
     for g in range(I // 4):
         parts = [proj[pl.ds(4 * g + a, SL, stride=I), :] for a in range(4)]
         tile = jnp.where(ln128 < 32, parts[0], jnp.where(ln128 < 64, parts[1],
                          jnp.where(ln128 < 96, parts[2], parts[3])))
         lall[mine, g * 128:(g + 1) * 128] = tile.astype(BF16)
 
-    pl.semaphore_wait(barrier, 4 + COLS - 1 + 2 - (across == c).astype(jnp.int32))
+    pl.semaphore_wait(barrier, 6 + COLS - 1 + 2 - (across == c).astype(jnp.int32))
 
     def hop_remote(src, dst, t, ss, rs):
         return pltpu.make_async_remote_copy(
@@ -182,24 +196,24 @@
         to = pl.ds(pl.multiple_of(k * 256, 256), 256)
         pr = jnp.concatenate([pair_ref[2 * k], pad, pair_ref[2 * k + 1], pad], axis=0)
         lo = jnp.concatenate([loss_ref[2 * k], pad, loss_ref[2 * k + 1], pad], axis=0)
-        ct[:, to] = dot_nt(iden, pr).astype(BF16)
-        lob = dot_nt(iden, lo).astype(BF16)
+        ct[:, to] = pr.T
+        lob = lo.T
         lot[:, to] = lob
         hgs[:, to] = dot(s_ref[...], lob).astype(BF16)
         return 0
 
-    lax.fori_loop(0, 12, ahead, 0)
+    lax.fori_loop(0, 12, ahead, 0, unroll=6)
 
     for t in range(2):
         hop_wait(rhop.at[:, pl.ds(SK * t, SK), :], rin.at[t], t, hop_s, hop_r.at[t])
 
     ln16 = lanes((SK, 128))
     here = pl.ds(pl.multiple_of(r * SK, SK), SK)
+    loose = [sum((restore(*[rin[n, 3 * m + k].astype(F32) for k in range(3)]) for m in range(4)), []) for n in range(2)]
     for g in range(G8):
         tiles = []
         for k in range(2):
-            a = rin[0, 2 * g + k].astype(F32)
-            b = rin[1, 2 * g + k].astype(F32)
+            a, b = loose[0][2 * g + k], loose[1][2 * g + k]
             tiles.append(jnp.where(ln16 < 48, a, roll(b, 48)))
             tiles.append(jnp.where(ln16 < 48, roll(a, 64), roll(b, 112)))
         for k, tile in enumerate(pack4(*tiles)):
@@ -217,6 +231,12 @@
             send(sl(1, 1, 1), sl(1, 1, 1), ag_s.at[g, 3], ag_r.at[g, 3], to(-1)),
         ]
 
+    def gather_direct(sl, to, g):
+        return [send(sl(0, 0, 2), sl(0, 0, 2), ag_s.at[g, k], ag_r.at[g, k], to(d)) for k, d in enumerate((1, -1, 2))]
+
+    def scatter_direct(sl, into, to, g):
+        return [send(sl(d, 0, 2), into.at[k], rs_s.at[g, k], rs_r.at[g, k], to(d)) for k, d in enumerate((1, -1, 2))]
+
     def scatter_ring(sl, relay, main, to, g):
         return [
             send(sl(2, 0, 1), relay.at[0], rs_s.at[g, 0], rs_r.at[g, 0], to(1)),
@@ -244,32 +264,30 @@
 
     sibling = (r, c + 1 - 2 * core)
     STEPS = (0, -1, 1, 2)
-    first = [gather_ring(chunk(rm, k, k == 1, 0), along(k == 1), 5 * k) for k in range(2)]
+    first = [gather_direct(chunk(rm, k, k == 1, 0), along(k == 1), 5 * k) for k in range(2)]
     second = [[gather_ring(chunk(rm, k, k == 0, w), along(k == 0), 5 * k + 1 + n)
                for n, w in enumerate(STEPS)] for k in range(2)]
     l_ring = gather_ring(l_chunk(lall), to_x, 10)
     l_sibs = [send(l_chunk(lall)(w, 0, 2), l_chunk(lall)(w, 0, 2), sib_s.at[n], sib_r.at[n], sibling)
               for n, w in enumerate(STEPS)]
     for k in range(2):
-        first[k][0].start()
-        first[k][1].start()
+        for copy in first[k]:
+            copy.start()
     for k in range(2):
         second[k][0][0].start()
         second[k][0][1].start()
     l_ring[0].start()
     l_ring[1].start()
     l_sibs[0].start()
-    lax.fori_loop(12, 15, ahead, 0)
+    lax.fori_loop(12, 15, ahead, 0, unroll=3)
     for m in range(2):
         for k in range(2):
             first[k][m].wait_recv()
-            first[k][2 + m].start()
             second[k][1 + m][0].start()
             second[k][1 + m][1].start()
-    lax.fori_loop(15, 18, ahead, 0)
+    lax.fori_loop(15, 18, ahead, 0, unroll=3)
     for k in range(2):
         first[k][2].wait_recv()
-        first[k][3].wait_recv()
         second[k][3][0].start()
         second[k][3][1].start()
     for m in range(2):
@@ -282,15 +300,14 @@
                 second[k][n][m].wait_recv()
                 second[k][n][2 + m].start()
         if n < 2:
-            lax.fori_loop(18 + 3 * n, 21 + 3 * n, ahead, 0)
+            lax.fori_loop(18 + 3 * n, 21 + 3 * n, ahead, 0, unroll=3)
     l_ring[2].wait_recv()
     l_ring[3].wait_recv()
     l_sibs[3].start()
     for n in range(4):
         l_sibs[n].wait_recv()
-    e256 = eye(S)
     for k in range(I * Q // S):
-        lt[k * S:(k + 1) * S, :] = dot_nt(e256, lall[:, k * S:(k + 1) * S]).astype(BF16)
+        lt[k * S:(k + 1) * S, :] = lall[:, k * S:(k + 1) * S].T
     for n in range(4):
         for k in range(2):
             second[k][n][2].wait_recv()
@@ -312,22 +329,29 @@
 
     scale = 1.0 / S
 
+    def mix(b, _):
+        for k in range(2):
+            at = pl.multiple_of((2 * b + k) * 256, 256)
+            ltb = lt[pl.ds(at, 256), :]
+            for ch in range(8):
+                d = dot(ltb, rm[:, ch * 512:(ch + 1) * 512]).astype(BF16)
+                for m in range(4):
+                    slab = ch * 4 + m
+                    for i in range(8):
+                        xs[k, slab * Q:(slab + 1) * Q, i * JP:(i + 1) * JP] = d[i * Q:(i + 1) * Q, m * 128:(m + 1) * 128]
+        for k in range(2):
+            to = pl.ds(pl.multiple_of((2 * b + k) * 1024, 1024), 1024)
+            ct[:, to] = (ct[:, to].astype(F32) + dot(wt[...], xs[k]) * scale).astype(BF16)
+        return 0
+
+    lax.fori_loop(0, I // 16, mix, 0)
+
     def block(t, _):
         ib = lax.rem(c + 1 + t, COLS)
-        ip = pl.ds(pl.multiple_of(ib * (IB * Q), IB * Q), IB * Q)
-        ltb = lt[ip, :]
-        for ch in range(8):
-            d = dot(ltb, rm[:, ch * 512:(ch + 1) * 512]).astype(BF16)
-            for k in range(4):
-                slab = ch * 4 + k
-                for i in range(IB):
-                    xs[slab * Q:(slab + 1) * Q, i * JP:(i + 1) * JP] = d[i * Q:(i + 1) * Q, k * 128:(k + 1) * 128]
         for half_block in range(IB // 2):
             i0 = ib * IB + 2 * half_block
-            ls = slice(half_block * 256, half_block * 256 + 256)
-            upd = dot(wt[...], xs[:, ls]) * scale
             here_l = pl.ds(pl.multiple_of(i0 * JP, 2 * JP), 2 * JP)
-            mid = (ct[:, here_l].astype(F32) + upd).astype(BF16).astype(F32)
+            mid = ct[:, here_l].astype(F32)
             center = mid - jnp.mean(mid, axis=0, keepdims=True)
             inv = lax.rsqrt(jnp.mean(center * center, axis=0, keepdims=True) + EPS)
             xn = center * inv
@@ -343,8 +367,8 @@
             gb = (lot[:, here_l].astype(F32) + (hatg - m1 - xn * m2) * inv).astype(BF16)
             for i in range(2):
                 sl = slice(i * JP, (i + 1) * JP)
-                obuf[i0 + i] = dot_nt(iden[0:J], outb[:, sl]).astype(BF16)
-                grad_ref[i0 + i] = dot_nt(iden[0:J], gb[:, sl]).astype(BF16)
+                obuf[i0 + i] = outb[:, sl].T[0:J]
+                grad_ref[i0 + i] = gb[:, sl].T[0:J]
             og = dot(wf[...], gb).astype(BF16)
             for i in range(2):
                 to = pl.ds(pl.multiple_of((i0 + i) * Q, Q), Q)
@@ -365,7 +389,7 @@
 
     big = [[scatter_ring(chunk(rgp, k, k == 0, w), r_relay.at[k, n], r_main.at[k, n], along(k == 0), 5 * k + n)
             for n, w in enumerate(STEPS)] for k in range(2)]
-    small = [scatter_ring(chunk(rgp, k, k == 1, 0), r_relay.at[k, 4], r_main.at[k, 4], along(k == 1), 5 * k + 4)
+    small = [scatter_direct(chunk(rgp, k, k == 1, 0), r_small.at[k], along(k == 1), 5 * k + 4)
              for k in range(2)]
     for g in range(0, G8, 2):
         a = dot(lall[...], ogs[:, 3 * g * 128:(3 * g + 6) * 128])
@@ -388,8 +412,7 @@
         dst[...] = tot.astype(BF16)
 
     def left_grad(k):
-        part = dot(ogs[k * S:(k + 1) * S, :], rmt[...]).astype(BF16)
-        lgt[:, k * S:(k + 1) * S] = dot_nt(e256, part).astype(BF16)
+        lgt[:, k * S:(k + 1) * S] = dot_nt(rm[...], ogs[k * S:(k + 1) * S, :]).astype(BF16)
 
     def relayed(ring, sl, relay):
         ring[0].wait_recv()
@@ -399,8 +422,6 @@
         add(sl(-1, 1, 1), relay.at[1])
         ring[3].start()
 
-    for ch in range(FULL // S):
-        rmt[ch * S:(ch + 1) * S, :] = dot_nt(e256, rm[:, ch * S:(ch + 1) * S]).astype(BF16)
     left_grad(0)
     for n, w in enumerate(STEPS):
         for k in range(2):
@@ -417,32 +438,37 @@
             big[k][n][3].wait_recv()
             add(chunk(rgp, k, k == 0, w)(0, 0, 2), r_main.at[k, n, 0], r_main.at[k, n, 1])
     for k in range(2):
-        small[k][0].start()
-        small[k][1].start()
+        for copy in small[k]:
+            copy.start()
     for n in range(4):
         l_swap[n].wait_recv()
         add(lgt.at[pl.ds(pl.multiple_of((2 * n + core) * SL, SL), SL)], l_sib.at[n])
     l_back = scatter_ring(l_chunk(lgt), l_relay, l_main, to_x, 10)
     l_back[0].start()
     l_back[1].start()
-    for k in range(2):
-        relayed(small[k], chunk(rgp, k, k == 1, 0), r_relay.at[k, 4])
     relayed(l_back, l_chunk(lgt), l_relay)
     for k in range(2):
-        small[k][2].wait_recv()
-        small[k][3].wait_recv()
+        for copy in small[k]:
+            copy.wait_recv()
+    loose = [[], []]
     for g in range(G8):
         tiles = []
         for m in range(3):
             at = (3 * g + m) * 128
             k, sl = at // (PK // 2), slice(at % (PK // 2), at % (PK // 2) + 128)
-            tiles.append(rgp[here, at:at + 128].astype(F32) + r_main[k, 4, 0, :, sl].astype(F32)
-                         + r_main[k, 4, 1, :, sl].astype(F32))
+            tot = rgp[here, at:at + 128].astype(F32)
+            for n in range(3):
+                tot = tot + r_small[k, n, :, sl].astype(F32)
+            tiles.append(tot)
         tiles.append(unpack_fourth(*tiles))
         for k in range(2):
             even, odd = tiles[2 * k], tiles[2 * k + 1]
-            rh[0, 2 * g + k] = jnp.where(ln16 < 64, even, roll(odd, 64)).astype(BF16)
-            rh[1, 2 * g + k] = jnp.where(ln16 < 64, roll(even, 80), roll(odd, 16)).astype(BF16)
+            loose[0].append(jnp.where(ln16 < 64, even, roll(odd, 64)))
+            loose[1].append(jnp.where(ln16 < 64, roll(even, 80), roll(odd, 16)))
+    for n in range(2):
+        for m in range(4):
+            for k, tile in enumerate(squeeze(*loose[n][4 * m:4 * m + 4])):
+                rh[n, 3 * m + k] = tile.astype(BF16)
     for t in range(2):
         hop_start(rh.at[t], rhin.at[half], t, hop2_s, hop2_r.at[half])
     l_back[2].wait_recv()
@@ -459,10 +485,12 @@
                 hg[k, pl.ds(4 * g + a, SL, stride=I), :] = res[a * SL:(a + 1) * SL, k * 128:(k + 1) * 128]
     for t in range(2):
         hop_wait(rh.at[t], rhin.at[t], t, hop2_s, hop2_r.at[t])
-    for qp in range(Q // 2):
-        both = jnp.concatenate([rhin[0, qp], rhin[1, qp]], axis=0).astype(F32)
-        tq[pl.ds(2 * qp, SL, stride=Q), :] = both
-        tq[pl.ds(2 * qp + 1, SL, stride=Q), :] = roll(both, 64)
+    for m in range(4):
+        dense = [jnp.concatenate([rhin[0, 3 * m + k], rhin[1, 3 * m + k]], axis=0).astype(F32) for k in range(3)]
+        for k, both in enumerate(restore(*dense)):
+            qp = 4 * m + k
+            tq[pl.ds(2 * qp, SL, stride=Q), :] = both
+            tq[pl.ds(2 * qp + 1, SL, stride=Q), :] = roll(both, 64)
     iden_i = eye(I, 128)
     lni = lanes((I, 128))
 
@@ -516,10 +544,10 @@
             pltpu.VMEM((SL * Q, 128), F32),
             pltpu.VMEM((S, I * Q), BF16),
             pltpu.VMEM((I * Q, S), BF16),
-            pltpu.VMEM((Q // 2, SL, 128), BF16),
-            pltpu.VMEM((2, Q // 2, SK, 128), BF16),
+            pltpu.VMEM((12, SL, 128), BF16),
+            pltpu.VMEM((2, 12, SK, 128), BF16),
             pltpu.VMEM((S, FULL), BF16),
-            pltpu.VMEM((Q * Q, IB * JP), BF16),
+            pltpu.VMEM((2, Q * Q, 8 * JP), BF16),
             pltpu.VMEM((I * Q, FULL), BF16),
             pltpu.VMEM((I, J, C), BF16),
             pltpu.VMEM((Q * Q, C), F32),
@@ -529,15 +557,15 @@
             pltpu.VMEM((C, H), BF16),
             pltpu.VMEM((S, I * Q), BF16),
             pltpu.VMEM((S, PK), BF16),
-            pltpu.VMEM((2, Q // 2, SK, 128), BF16),
-            pltpu.VMEM((2, Q // 2, SK, 128), BF16),
+            pltpu.VMEM((2, 12, SK, 128), BF16),
+            pltpu.VMEM((2, 12, SK, 128), BF16),
             pltpu.VMEM((2, SL * I, 128), F32),
             pltpu.VMEM((C, I * JP), BF16),
             pltpu.VMEM((C, I * JP), BF16),
             pltpu.VMEM((H, I * JP), BF16),
-            pltpu.VMEM((FULL, S), BF16),
-            pltpu.VMEM((2, 5, 2, SK, PK // 4), BF16),
-            pltpu.VMEM((2, 5, 2, SK, PK // 2), BF16),
+            pltpu.VMEM((2, 4, 2, SK, PK // 4), BF16),
+            pltpu.VMEM((2, 4, 2, SK, PK // 2), BF16),
+            pltpu.VMEM((2, 3, SK, PK // 2), BF16),
             pltpu.VMEM((2, SL, I * Q // 2), BF16),
             pltpu.VMEM((2, SL, I * Q), BF16),
             pltpu.VMEM((4, SL, I * Q), BF16),

time: 108 us -> 92.7 us (0.86)
  Pallas kernels: 101 us -> 86.5 us
    pallas_call x1, Pallas kernels: 101 us -> 86.5 us  [on_device(): pl.pallas_call(kernel, out_shape=(jax.ShapeDtypeStruct((IB, J * COLS, C),...]
where the time goes in v3:
time: 92.7 us; the launch traced here: 92 us
  Pallas kernels  86.5 us (93%)
  local copies, waits for them, and re-layouts  4.9 us (5%)
    pallas_call x1, Pallas kernels, on_device(): pl.pallas_call(kernel, out_shape=(jax.ShapeDtypeStruct((IB, J * COLS, C),...  86.5 us
    unnamed x7, local copies, waits for them, and re-layouts  4.9 us

profile of v3, /device:TPU:7, one launch (start us, length us, event | category | flops | bytes accessed | tf_op | source)
XLA Modules:
  0.0 92.0 jit_solution(13235260528440868782)
XLA Ops:
  0.6 86.5 %shard_map.103 = (bf16[6,768,128]{2,1,0:T(8,128)(2,1)}, bf16[48,96,128]{2,1,0:T(8,128)(2,1)}, bf16[32,48,256]{2,1,0:T(8,128)(2,1)}) custom-call(bf16[32,48,256]{2,1,0:T(8,128)(2,1)} %x_ref.1, bf16[48,96,128]{2,1,0:T(8,128)(2,1)} %pair_ref.1, bf16[48,96,128]{2,1,0:T(8,128)(2,1)} %loss_ref.1, bf16[32,256]{1,0:T(8,128)(2,1)} %bitcast.2, ...), custom_call_target="tpu_custom_call" | custom-call | flops 16000000000 | bytes 8000000 | tf_op jit(solution)/shard_map/pallas_call | solution.py:531
  87.1 0.0 copy-start
  87.1 2.5 %copy.14 = bf16[6,768,128]{2,1,0:T(8,128)(2,1)} copy(bf16[6,768,128]{2,1,0:T(8,128)(2,1)} %get-tuple-element.6) | data formatting | bytes 2359296
  89.6 0.0 copy-done
  89.6 0.0 copy-start.1
  89.6 1.0 %copy.15 = bf16[48,96,128]{2,1,0:T(8,128)(2,1)} copy(bf16[48,96,128]{2,1,0:T(8,128)(2,1)S(1)} %copy-done) | data formatting | bytes 2359296
  90.6 0.5 copy-done.1
  91.1 0.9 copy.16
Async XLA Ops:
  87.1 2.5 %copy-start = (bf16[48,96,128]{2,1,0:T(8,128)(2,1)S(1)}, bf16[48,96,128]{2,1,0:T(8,128)(2,1)}, u32[]{:S(2)}) copy-start(bf16[48,96,128]{2,1,0:T(8,128)(2,1)} %get-tuple-element.7) | copy-start | bytes 3538948
  89.6 1.6 %copy-start.1 = (bf16[32,48,256]{2,1,0:T(8,128)(2,1)S(1)}, bf16[32,48,256]{2,1,0:T(8,128)(2,1)}, u32[]{:S(2)}) copy-start(bf16[32,48,256]{2,1,0:T(8,128)(2,1)} %get-tuple-element.8) | copy-start | bytes 2359300

commit v4 on v3

--- a/solution.py
+++ b/solution.py
@@ -22,7 +22,19 @@
 PK = 3 * G8 * 128
 FULL = Q * JP
 IB = I // COLS
-SLABS = [4 * (k // 3) + k % 3 for k in range(3 * G8)] + [4 * g + 3 for g in range(G8)]
+HALF = FULL // 2
+SLABS = sum(([4 * g + m for g in range(4 * k, 4 * k + 4) for m in range(3)]
+             + [4 * g + 3 for g in range(4 * k, 4 * k + 4)] for k in range(2)), [])
+
+
+def packed(g, m):
+    at = (g // 4) * HALF + (3 * (g % 4) + m) * 128
+    return slice(at, at + 128)
+
+
+def fourth(g):
+    at = (g // 4) * HALF + (12 + g % 4) * 128
+    return slice(at, at + 128)
 
 
 def dot(a, b):
@@ -75,7 +87,7 @@
 def kernel(
     x_ref, pair_ref, loss_ref, f_ref, g_ref, w_ref, e_ref, s_ref,
     out_ref, grad_ref, slope_ref,
-    xhat, rstd, proj, tq, lall, lt, rhop, rin, rm, xs, ogs, obuf,
+    xhat, rstd, proj, tq, lall, lt, rhop, rin, rm, xs, acc, ogs, obuf,
     wf32, wf, wt, et, st, lgt, rgp, rh, rhin, hg, ct, lot, hgs, r_relay, r_main, r_small, l_relay, l_main, l_sib,
     hop_s, hop_r, ag_s, ag_r, sib_s, sib_r, a2a_s, a2a_r, rs_s, rs_r, hop2_s, hop2_r,
 ):
@@ -134,7 +146,7 @@
             tq[pl.ds(to, Q), 0:I] = dot_nt(g_ref[...], xb[k * I:(k + 1) * I])
         return 0
 
-    lax.fori_loop(0, SL // 4, project, 0)
+    lax.fori_loop(0, SL // 4, project, 0, unroll=4)
 
     mine = pl.ds(pl.multiple_of(c * SL, SL), SL)
     for m in range(4):
@@ -155,7 +167,7 @@
 
     def hop_remote(src, dst, t, ss, rs):
         return pltpu.make_async_remote_copy(
-            src_ref=src, dst_ref=dst, send_sem=ss.at[t], recv_sem=rs,
+            src_ref=src, dst_ref=dst, send_sem=ss, recv_sem=rs,
             device_id=(2 * c + t, across), device_id_type=MESH)
 
     def hop_start(src, dst, t, ss, rs):
@@ -181,8 +193,23 @@
         def _():
             hop_remote(src, dst, t, ss, rs).wait_send()
 
-    for t in range(2):
-        hop_start(rhop.at[:, pl.ds(SK * t, SK), :], rin.at[half], t, hop_s, hop_r.at[half])
+    def hop_out(k, t):
+        return (rhop.at[pl.ds(6 * k, 6), pl.ds(SK * t, SK), :], rin.at[half, pl.ds(6 * k, 6)], t,
+                hop_s.at[k, t], hop_r.at[k, half])
+
+    def hop_in(k, t):
+        return (rhop.at[pl.ds(6 * k, 6), pl.ds(SK * t, SK), :], rin.at[t, pl.ds(6 * k, 6)], t,
+                hop_s.at[k, t], hop_r.at[k, t])
+
+    def back_out(k, t):
+        return (rh.at[t, pl.ds(6 * k, 6)], rhin.at[half, pl.ds(6 * k, 6)], t, hop2_s.at[k, t], hop2_r.at[k, half])
+
+    def back_in(k, t):
+        return (rh.at[t, pl.ds(6 * k, 6)], rhin.at[t, pl.ds(6 * k, 6)], t, hop2_s.at[k, t], hop2_r.at[k, t])
+
+    for k in range(2):
+        for t in range(2):
+            hop_start(*hop_out(k, t))
 
     wf32[...] = w_ref[...].astype(F32)
     for k, q in enumerate(SLABS):
@@ -204,20 +231,20 @@
 
     lax.fori_loop(0, 12, ahead, 0, unroll=6)
 
-    for t in range(2):
-        hop_wait(rhop.at[:, pl.ds(SK * t, SK), :], rin.at[t], t, hop_s, hop_r.at[t])
-
     ln16 = lanes((SK, 128))
     here = pl.ds(pl.multiple_of(r * SK, SK), SK)
-    loose = [sum((restore(*[rin[n, 3 * m + k].astype(F32) for k in range(3)]) for m in range(4)), []) for n in range(2)]
-    for g in range(G8):
-        tiles = []
-        for k in range(2):
-            a, b = loose[0][2 * g + k], loose[1][2 * g + k]
-            tiles.append(jnp.where(ln16 < 48, a, roll(b, 48)))
-            tiles.append(jnp.where(ln16 < 48, roll(a, 64), roll(b, 112)))
-        for k, tile in enumerate(pack4(*tiles)):
-            rm[here, (3 * g + k) * 128:(3 * g + k + 1) * 128] = tile.astype(BF16)
+
+    def assemble(k):
+        loose = [sum((restore(*[rin[n, 3 * m + i].astype(F32) for i in range(3)]) for m in (2 * k, 2 * k + 1)), [])
+                 for n in range(2)]
+        for g in range(4):
+            tiles = []
+            for i in range(2):
+                a, b = loose[0][2 * g + i], loose[1][2 * g + i]
+                tiles.append(jnp.where(ln16 < 48, a, roll(b, 48)))
+                tiles.append(jnp.where(ln16 < 48, roll(a, 64), roll(b, 112)))
+            for m, tile in enumerate(pack4(*tiles)):
+                rm[here, packed(4 * k + g, m)] = tile.astype(BF16)
 
     def send(src, dst, ss, rs, to):
         return pltpu.make_async_remote_copy(
@@ -248,7 +275,8 @@
     def chunk(ref, side, along_z, w):
         def sl(off, first, count):
             row = at_row(z + off, y + w) if along_z else at_row(z + w, y + off)
-            return ref.at[pl.ds(pl.multiple_of(row * SK, SK), SK), pl.ds(side * (PK // 2) + first * (PK // 4), count * (PK // 4))]
+            return ref.at[pl.ds(pl.multiple_of(row * SK, SK), SK),
+                          pl.ds(side * (HALF if ref is rm else PK // 2) + first * (PK // 4), count * (PK // 4))]
         return sl
 
     def along(along_z):
@@ -271,36 +299,31 @@
     l_sibs = [send(l_chunk(lall)(w, 0, 2), l_chunk(lall)(w, 0, 2), sib_s.at[n], sib_r.at[n], sibling)
               for n, w in enumerate(STEPS)]
     for k in range(2):
-        for copy in first[k]:
+        for t in range(2):
+            hop_wait(*hop_in(k, t))
+        assemble(k)
+        for copy in first[k] + second[k][0][:2]:
             copy.start()
-    for k in range(2):
-        second[k][0][0].start()
-        second[k][0][1].start()
     l_ring[0].start()
     l_ring[1].start()
     l_sibs[0].start()
     lax.fori_loop(12, 15, ahead, 0, unroll=3)
-    for m in range(2):
-        for k in range(2):
+    for k in range(2):
+        for m in range(3):
             first[k][m].wait_recv()
             second[k][1 + m][0].start()
             second[k][1 + m][1].start()
     lax.fori_loop(15, 18, ahead, 0, unroll=3)
-    for k in range(2):
-        first[k][2].wait_recv()
-        second[k][3][0].start()
-        second[k][3][1].start()
     for m in range(2):
         l_ring[m].wait_recv()
         l_ring[2 + m].start()
         l_sibs[1 + m].start()
-    for n in range(4):
-        for m in range(2):
-            for k in range(2):
+    for k in range(2):
+        for n in range(4):
+            for m in range(2):
                 second[k][n][m].wait_recv()
                 second[k][n][2 + m].start()
-        if n < 2:
-            lax.fori_loop(18 + 3 * n, 21 + 3 * n, ahead, 0, unroll=3)
+        lax.fori_loop(18 + 3 * k, 21 + 3 * k, ahead, 0, unroll=3)
     l_ring[2].wait_recv()
     l_ring[3].wait_recv()
     l_sibs[3].start()
@@ -308,43 +331,45 @@
         l_sibs[n].wait_recv()
     for k in range(I * Q // S):
         lt[k * S:(k + 1) * S, :] = lall[:, k * S:(k + 1) * S].T
-    for n in range(4):
-        for k in range(2):
-            second[k][n][2].wait_recv()
-            second[k][n][3].wait_recv()
-    for g in range(G8):
-        t0, t1, t2 = [rm[:, (3 * g + k) * 128:(3 * g + k + 1) * 128].astype(F32) for k in range(3)]
-        rm[:, (3 * G8 + g) * 128:(3 * G8 + g + 1) * 128] = unpack_fourth(t0, t1, t2).astype(BF16)
-
-    def a2a_copy(t):
-        to = lax.rem(c + 1 + t, COLS)
-        return pltpu.make_async_remote_copy(
-            src_ref=obuf.at[pl.ds(to * IB, IB)], dst_ref=out_ref.at[:, pl.ds(pl.multiple_of(c * J, J), J), :],
-            send_sem=a2a_s.at[t], recv_sem=a2a_r.at[t], device_id=(r, to), device_id_type=MESH)
-
-    def own_copy():
-        return pltpu.make_async_copy(
-            obuf.at[pl.ds(c * IB, IB)], out_ref.at[:, pl.ds(pl.multiple_of(c * J, J), J), :],
-            a2a_s.at[COLS - 1])
-
     scale = 1.0 / S
 
-    def mix(b, _):
+    def mix(side, b):
         for k in range(2):
             at = pl.multiple_of((2 * b + k) * 256, 256)
             ltb = lt[pl.ds(at, 256), :]
-            for ch in range(8):
-                d = dot(ltb, rm[:, ch * 512:(ch + 1) * 512]).astype(BF16)
+            for ch in range(4):
+                d = dot(ltb, rm[:, side * HALF + ch * 512:side * HALF + (ch + 1) * 512]).astype(BF16)
                 for m in range(4):
                     slab = ch * 4 + m
                     for i in range(8):
                         xs[k, slab * Q:(slab + 1) * Q, i * JP:(i + 1) * JP] = d[i * Q:(i + 1) * Q, m * 128:(m + 1) * 128]
         for k in range(2):
             to = pl.ds(pl.multiple_of((2 * b + k) * 1024, 1024), 1024)
-            ct[:, to] = (ct[:, to].astype(F32) + dot(wt[...], xs[k]) * scale).astype(BF16)
+            part = dot(wt[:, side * 512:(side + 1) * 512], xs[k])
+            if side == 0:
+                acc[:, to] = part
+            else:
+                ct[:, to] = (ct[:, to].astype(F32) + (acc[:, to] + part) * scale).astype(BF16)
         return 0
 
-    lax.fori_loop(0, I // 16, mix, 0)
+    for k in range(2):
+        for n in range(4):
+            second[k][n][2].wait_recv()
+            second[k][n][3].wait_recv()
+        for g in range(4 * k, 4 * k + 4):
+            rm[:, fourth(g)] = unpack_fourth(*[rm[:, packed(g, m)].astype(F32) for m in range(3)]).astype(BF16)
+        lax.fori_loop(0, I // 16, lambda b, _: mix(k, b), 0)
+
+    def a2a_copy(t):
+        to = lax.rem(c + 1 + t, COLS)
+        return pltpu.make_async_remote_copy(
+            src_ref=obuf.at[pl.ds(to * IB, IB)], dst_ref=out_ref.at[:, pl.ds(pl.multiple_of(c * J, J), J), :],
+            send_sem=a2a_s.at[t], recv_sem=a2a_r.at[t], device_id=(r, to), device_id_type=MESH)
+
+    def own_copy():
+        return pltpu.make_async_copy(
+            obuf.at[pl.ds(c * IB, IB)], out_ref.at[:, pl.ds(pl.multiple_of(c * J, J), J), :],
+            a2a_s.at[COLS - 1])
 
     def block(t, _):
         ib = lax.rem(c + 1 + t, COLS)
@@ -385,15 +410,15 @@
 
         return 0
 
-    lax.fori_loop(0, COLS, block, 0)
+    lax.fori_loop(0, COLS, block, 0, unroll=2)
 
     big = [[scatter_ring(chunk(rgp, k, k == 0, w), r_relay.at[k, n], r_main.at[k, n], along(k == 0), 5 * k + n)
             for n, w in enumerate(STEPS)] for k in range(2)]
     small = [scatter_direct(chunk(rgp, k, k == 1, 0), r_small.at[k], along(k == 1), 5 * k + 4)
              for k in range(2)]
     for g in range(0, G8, 2):
-        a = dot(lall[...], ogs[:, 3 * g * 128:(3 * g + 6) * 128])
-        b = dot(lall[...], ogs[:, (3 * G8 + g) * 128:(3 * G8 + g + 2) * 128])
+        a = dot(lall[...], ogs[:, packed(g, 0).start:packed(g + 1, 2).stop])
+        b = dot(lall[...], ogs[:, fourth(g).start:fourth(g + 1).stop])
         for k in range(2):
             tiles = pack4(*[a[:, (3 * k + m) * 128:(3 * k + m + 1) * 128] for m in range(3)],
                           b[:, k * 128:(k + 1) * 128])
@@ -432,12 +457,11 @@
                    sib_s.at[4 + n], sib_r.at[4 + n], sibling) for n in range(4)]
     for n in range(4):
         l_swap[n].start()
-    for n, w in reversed(list(enumerate(STEPS))):
-        for k in range(2):
+    for k in range(2):
+        for n, w in enumerate(STEPS):
             big[k][n][2].wait_recv()
             big[k][n][3].wait_recv()
             add(chunk(rgp, k, k == 0, w)(0, 0, 2), r_main.at[k, n, 0], r_main.at[k, n, 1])
-    for k in range(2):
         for copy in small[k]:
             copy.start()
     for n in range(4):
@@ -446,31 +470,35 @@
     l_back = scatter_ring(l_chunk(lgt), l_relay, l_main, to_x, 10)
     l_back[0].start()
     l_back[1].start()
-    relayed(l_back, l_chunk(lgt), l_relay)
-    for k in range(2):
+
+    def hand_back(k):
         for copy in small[k]:
             copy.wait_recv()
-    loose = [[], []]
-    for g in range(G8):
-        tiles = []
-        for m in range(3):
-            at = (3 * g + m) * 128
-            k, sl = at // (PK // 2), slice(at % (PK // 2), at % (PK // 2) + 128)
-            tot = rgp[here, at:at + 128].astype(F32)
-            for n in range(3):
-                tot = tot + r_small[k, n, :, sl].astype(F32)
-            tiles.append(tot)
-        tiles.append(unpack_fourth(*tiles))
-        for k in range(2):
-            even, odd = tiles[2 * k], tiles[2 * k + 1]
-            loose[0].append(jnp.where(ln16 < 64, even, roll(odd, 64)))
-            loose[1].append(jnp.where(ln16 < 64, roll(even, 80), roll(odd, 16)))
-    for n in range(2):
-        for m in range(4):
-            for k, tile in enumerate(squeeze(*loose[n][4 * m:4 * m + 4])):
-                rh[n, 3 * m + k] = tile.astype(BF16)
-    for t in range(2):
-        hop_start(rh.at[t], rhin.at[half], t, hop2_s, hop2_r.at[half])
+        loose = [[], []]
+        for g in range(4 * k, 4 * k + 4):
+            tiles = []
+            for m in range(3):
+                at = (3 * g + m) * 128
+                sl = slice(at - k * (PK // 2), at - k * (PK // 2) + 128)
+                tot = rgp[here, at:at + 128].astype(F32)
+                for n in range(3):
+                    tot = tot + r_small[k, n, :, sl].astype(F32)
+                tiles.append(tot)
+            tiles.append(unpack_fourth(*tiles))
+            for i in range(2):
+                even, odd = tiles[2 * i], tiles[2 * i + 1]
+                loose[0].append(jnp.where(ln16 < 64, even, roll(odd, 64)))
+                loose[1].append(jnp.where(ln16 < 64, roll(even, 80), roll(odd, 16)))
+        for n in range(2):
+            for m in range(2):
+                for i, tile in enumerate(squeeze(*loose[n][4 * m:4 * m + 4])):
+                    rh[n, 6 * k + 3 * m + i] = tile.astype(BF16)
+        for t in range(2):
+            hop_start(*back_out(k, t))
+
+    hand_back(0)
+    relayed(l_back, l_chunk(lgt), l_relay)
+    hand_back(1)
     l_back[2].wait_recv()
     l_back[3].wait_recv()
     zero = jnp.zeros((SL, 128), F32)
@@ -483,8 +511,9 @@
         for a in range(4):
             for k in range(2):
                 hg[k, pl.ds(4 * g + a, SL, stride=I), :] = res[a * SL:(a + 1) * SL, k * 128:(k + 1) * 128]
-    for t in range(2):
-        hop_wait(rh.at[t], rhin.at[t], t, hop2_s, hop2_r.at[t])
+    for k in range(2):
+        for t in range(2):
+            hop_wait(*back_in(k, t))
     for m in range(4):
         dense = [jnp.concatenate([rhin[0, 3 * m + k], rhin[1, 3 * m + k]], axis=0).astype(F32) for k in range(3)]
         for k, both in enumerate(restore(*dense)):
@@ -509,7 +538,7 @@
         slope_ref[pl.ds(b * 4, 4)] = res.astype(BF16).reshape(4, I, CH)
         return 0
 
-    lax.fori_loop(0, SL // 4, finish, 0)
+    lax.fori_loop(0, SL // 4, finish, 0, unroll=4)
 
     def drain(t, _):
         a2a_copy(t).wait()
@@ -520,9 +549,10 @@
         for copy in ring:
             copy.wait_send()
     own_copy().wait()
-    for t in range(2):
-        hop_sent(rhop.at[:, pl.ds(SK * t, SK), :], rin.at[half], t, hop_s, hop_r.at[half])
-        hop_sent(rh.at[t], rhin.at[half], t, hop2_s, hop2_r.at[half])
+    for k in range(2):
+        for t in range(2):
+            hop_sent(*hop_out(k, t))
+            hop_sent(*back_out(k, t))
 
 
 def on_device(profile, pair, loss, former, latter, mixing, expand, shrink):
@@ -547,7 +577,8 @@
             pltpu.VMEM((12, SL, 128), BF16),
             pltpu.VMEM((2, 12, SK, 128), BF16),
             pltpu.VMEM((S, FULL), BF16),
-            pltpu.VMEM((2, Q * Q, 8 * JP), BF16),
+            pltpu.VMEM((2, Q * Q // 2, 8 * JP), BF16),
+            pltpu.VMEM((C, I * JP), F32),
             pltpu.VMEM((I * Q, FULL), BF16),
             pltpu.VMEM((I, J, C), BF16),
             pltpu.VMEM((Q * Q, C), F32),
@@ -569,12 +600,12 @@
             pltpu.VMEM((2, SL, I * Q // 2), BF16),
             pltpu.VMEM((2, SL, I * Q), BF16),
             pltpu.VMEM((4, SL, I * Q), BF16),
-            dma((2,)), dma((2,)),
+            dma((2, 2)), dma((2, 2)),
             dma((11, 4)), dma((11, 4)),
             dma((8,)), dma((8,)),
             dma((COLS,)), dma((COLS,)),
             dma((11, 4)), dma((11, 4)),
-            dma((2,)), dma((2,)),
+            dma((2, 2)), dma((2, 2)),
         ],
         compiler_params=pltpu.CompilerParams(
             collective_id=0, has_side_effects=True, vmem_limit_bytes=60 * 1024 * 1024),

time: 92.7 us -> 90.2 us (0.973)
  Pallas kernels: 86.5 us -> 84.4 us
    pallas_call x1, Pallas kernels: 86.5 us -> 84.4 us  [on_device(): pl.pallas_call(kernel, out_shape=(jax.ShapeDtypeStruct((IB, J * COLS, C),...]
where the time goes in v4:
time: 90.2 us; the launch traced here: 90 us
  Pallas kernels  84.4 us (94%)
  local copies, waits for them, and re-layouts  4.9 us (5%)
    pallas_call x1, Pallas kernels, on_device(): pl.pallas_call(kernel, out_shape=(jax.ShapeDtypeStruct((IB, J * COLS, C),...  84.4 us
    unnamed x7, local copies, waits for them, and re-layouts  4.9 us

profile of v4, /device:TPU:7, one launch (start us, length us, event | category | flops | bytes accessed | tf_op | source)
XLA Modules:
  0.0 90.0 jit_solution(14814016619535157070)
XLA Ops:
  0.6 84.4 %shard_map.103 = (bf16[6,768,128]{2,1,0:T(8,128)(2,1)}, bf16[48,96,128]{2,1,0:T(8,128)(2,1)}, bf16[32,48,256]{2,1,0:T(8,128)(2,1)}) custom-call(bf16[32,48,256]{2,1,0:T(8,128)(2,1)} %x_ref.1, bf16[48,96,128]{2,1,0:T(8,128)(2,1)} %pair_ref.1, bf16[48,96,128]{2,1,0:T(8,128)(2,1)} %loss_ref.1, bf16[32,256]{1,0:T(8,128)(2,1)} %bitcast.2, ...), custom_call_target="tpu_custom_call" | custom-call | flops 16000000000 | bytes 8000000 | tf_op jit(solution)/shard_map/pallas_call | solution.py:561
  85.1 0.0 copy-start
  85.1 2.5 %copy.14 = bf16[6,768,128]{2,1,0:T(8,128)(2,1)} copy(bf16[6,768,128]{2,1,0:T(8,128)(2,1)} %get-tuple-element.6) | data formatting | bytes 2359296
  87.5 0.0 copy-done
  87.5 0.0 copy-start.1
  87.5 1.0 %copy.15 = bf16[48,96,128]{2,1,0:T(8,128)(2,1)} copy(bf16[48,96,128]{2,1,0:T(8,128)(2,1)S(1)} %copy-done) | data formatting | bytes 2359296
  88.6 0.5 copy-done.1
  89.1 0.9 copy.16
Async XLA Ops:
  85.1 2.5 %copy-start = (bf16[48,96,128]{2,1,0:T(8,128)(2,1)S(1)}, bf16[48,96,128]{2,1,0:T(8,128)(2,1)}, u32[]{:S(2)}) copy-start(bf16[48,96,128]{2,1,0:T(8,128)(2,1)} %get-tuple-element.7) | copy-start | bytes 3538948
  87.5 1.6 %copy-start.1 = (bf16[32,48,256]{2,1,0:T(8,128)(2,1)S(1)}, bf16[32,48,256]{2,1,0:T(8,128)(2,1)}, u32[]{:S(2)}) copy-start(bf16[32,48,256]{2,1,0:T(8,128)(2,1)} %get-tuple-element.8) | copy-start | bytes 2359300

commit v5 on v4

--- a/solution.py
+++ b/solution.py
@@ -84,12 +84,25 @@
     return jnp.where(ln < 32, roll(t0, 32), jnp.where(ln < 64, roll(t1, 64), roll(t2, 96)))
 
 
+def tile_rows():
+    return jnp.where(
+        lax.rem(lax.broadcasted_iota(jnp.int32, (128, Q), 0), Q)
+        == lax.broadcasted_iota(jnp.int32, (128, Q), 1), 1.0, 0.0).astype(BF16)
+
+
+def normalise(x_ref, b):
+    xr = x_ref[pl.ds(b * 4, 4)].reshape(4 * I, CH).astype(F32)
+    center = xr - jnp.mean(xr, axis=-1, keepdims=True)
+    inv = lax.rsqrt(jnp.mean(center * center, axis=-1, keepdims=True) + EPS)
+    return center * inv, inv
+
+
 def kernel(
-    x_ref, pair_ref, loss_ref, f_ref, g_ref, w_ref, e_ref, s_ref,
-    out_ref, grad_ref, slope_ref,
-    xhat, rstd, proj, tq, lall, lt, rhop, rin, rm, xs, acc, ogs, obuf,
-    wf32, wf, wt, et, st, lgt, rgp, rh, rhin, hg, ct, lot, hgs, r_relay, r_main, r_small, l_relay, l_main, l_sib,
-    hop_s, hop_r, ag_s, ag_r, sib_s, sib_r, a2a_s, a2a_r, rs_s, rs_r, hop2_s, hop2_r,
+    x_ref, pair_hbm, loss_hbm, f_ref, g_ref, w_ref, e_ref, s_ref,
+    out_ref, grad_hbm, ltot_ref, tq_ref,
+    pair_ref, loss_ref, gbuf, proj, tq, lall, lt, rhop, rin, rm, xs, acc, ogs, obuf,
+    wf32, wf, wt, et, st, lgt, rgp, rh, rhin, ct, lot, hgs, r_relay, r_main, r_small, l_relay, l_main, l_sib,
+    io_s, hop_s, hop_r, ag_s, ag_r, sib_s, sib_r, a2a_s, a2a_r, rs_s, rs_r, hop2_s, hop2_r,
 ):
     r = lax.axis_index("row")
     c = lax.axis_index("col")
@@ -97,6 +110,9 @@
     across = lax.div(r, 2)
 
     z, y = lax.div(r, 4), lax.rem(r, 4)
+    fetch = [pltpu.make_async_copy(pair_hbm, pair_ref, io_s.at[0]), pltpu.make_async_copy(loss_hbm, loss_ref, io_s.at[1])]
+    for copy in fetch:
+        copy.start()
     x, core = lax.div(c, 2), lax.rem(c, 2)
 
     barrier = pltpu.get_barrier_semaphore()
@@ -123,22 +139,13 @@
 
     iden = eye(C)
     ln128 = lanes((SL, 128))
-    tile4 = jnp.where(
-        lax.rem(lax.broadcasted_iota(jnp.int32, (128, Q), 0), Q)
-        == lax.broadcasted_iota(jnp.int32, (128, Q), 1), 1.0, 0.0).astype(BF16)
-    f4t = dot(tile4, f_ref[...]).astype(BF16)
-    g4t = dot(tile4, g_ref[...]).astype(BF16)
+    f4t = dot(tile_rows(), f_ref[...]).astype(BF16)
     tq[...] = jnp.zeros_like(tq)
 
     def project(b, _):
         rows = 4 * I
         at = pl.multiple_of(b * rows, rows)
-        xr = x_ref[pl.ds(b * 4, 4)].reshape(rows, CH).astype(F32)
-        center = xr - jnp.mean(xr, axis=-1, keepdims=True)
-        inv = lax.rsqrt(jnp.mean(center * center, axis=-1, keepdims=True) + EPS)
-        xn = center * inv
-        xhat[pl.ds(at, rows), :] = xn
-        rstd[pl.ds(at, rows), :] = inv
+        xn = normalise(x_ref, b)[0]
         xb = xn.astype(BF16)
         proj[pl.ds(at, rows), :] = dot_nt(xb, f4t)
         for k in range(4):
@@ -218,6 +225,8 @@
     st[...] = dot_nt(iden, s_ref[...]).astype(BF16)
     et[...] = dot_nt(eye(H), e_ref[...]).astype(BF16)
     pad = jnp.zeros((JP - J, C), BF16)
+    for copy in fetch:
+        copy.wait()
 
     def ahead(k, _):
         to = pl.ds(pl.multiple_of(k * 256, 256), 256)
@@ -358,7 +367,7 @@
             second[k][n][3].wait_recv()
         for g in range(4 * k, 4 * k + 4):
             rm[:, fourth(g)] = unpack_fourth(*[rm[:, packed(g, m)].astype(F32) for m in range(3)]).astype(BF16)
-        lax.fori_loop(0, I // 16, lambda b, _: mix(k, b), 0)
+        lax.fori_loop(0, I // 16, lambda b, _: mix(k, b), 0, unroll=3)
 
     def a2a_copy(t):
         to = lax.rem(c + 1 + t, COLS)
@@ -373,32 +382,31 @@
 
     def block(t, _):
         ib = lax.rem(c + 1 + t, COLS)
-        for half_block in range(IB // 2):
-            i0 = ib * IB + 2 * half_block
-            here_l = pl.ds(pl.multiple_of(i0 * JP, 2 * JP), 2 * JP)
-            mid = ct[:, here_l].astype(F32)
-            center = mid - jnp.mean(mid, axis=0, keepdims=True)
-            inv = lax.rsqrt(jnp.mean(center * center, axis=0, keepdims=True) + EPS)
-            xn = center * inv
-            pre = dot(et[...], xn.astype(BF16))
-            hgr = hgs[:, here_l].astype(F32)
-            sg = 0.5 * jnp.tanh(0.5 * pre) + 0.5
-            hid = pre * sg
-            pgr = (hgr * (sg + hid * (1.0 - sg))).astype(BF16)
-            outb = (mid + dot(st[...], hid.astype(BF16))).astype(BF16)
-            hatg = dot(e_ref[...], pgr)
-            m1 = jnp.mean(hatg, axis=0, keepdims=True)
-            m2 = jnp.mean(hatg * xn, axis=0, keepdims=True)
-            gb = (lot[:, here_l].astype(F32) + (hatg - m1 - xn * m2) * inv).astype(BF16)
-            for i in range(2):
-                sl = slice(i * JP, (i + 1) * JP)
-                obuf[i0 + i] = outb[:, sl].T[0:J]
-                grad_ref[i0 + i] = gb[:, sl].T[0:J]
-            og = dot(wf[...], gb).astype(BF16)
-            for i in range(2):
-                to = pl.ds(pl.multiple_of((i0 + i) * Q, Q), Q)
-                for k in range(Q):
-                    ogs[to, k * 128:(k + 1) * 128] = og[k * Q:(k + 1) * Q, i * JP:(i + 1) * JP]
+        i0 = ib * IB
+        here_l = pl.ds(pl.multiple_of(i0 * JP, IB * JP), IB * JP)
+        mid = ct[:, here_l].astype(F32)
+        center = mid - jnp.mean(mid, axis=0, keepdims=True)
+        inv = lax.rsqrt(jnp.mean(center * center, axis=0, keepdims=True) + EPS)
+        xn = center * inv
+        pre = dot(et[...], xn.astype(BF16))
+        hgr = hgs[:, here_l].astype(F32)
+        sg = 0.5 * jnp.tanh(0.5 * pre) + 0.5
+        hid = pre * sg
+        pgr = (hgr * (sg + hid * (1.0 - sg))).astype(BF16)
+        outb = (mid + dot(st[...], hid.astype(BF16))).astype(BF16)
+        hatg = dot(e_ref[...], pgr)
+        m1 = jnp.mean(hatg, axis=0, keepdims=True)
+        m2 = jnp.mean(hatg * xn, axis=0, keepdims=True)
+        gb = (lot[:, here_l].astype(F32) + (hatg - m1 - xn * m2) * inv).astype(BF16)
+        for i in range(IB):
+            sl = slice(i * JP, (i + 1) * JP)
+            obuf[i0 + i] = outb[:, sl].T[0:J]
+            gbuf[i0 + i] = gb[:, sl].T[0:J]
+        og = dot(wf[...], gb).astype(BF16)
+        for i in range(IB):
+            to = pl.ds(pl.multiple_of((i0 + i) * Q, Q), Q)
+            for k in range(Q):
+                ogs[to, k * 128:(k + 1) * 128] = og[k * Q:(k + 1) * Q, i * JP:(i + 1) * JP]
 
         @pl.when(t < COLS - 1)
         def _():
@@ -411,6 +419,8 @@
         return 0
 
     lax.fori_loop(0, COLS, block, 0, unroll=2)
+    keep = pltpu.make_async_copy(gbuf, grad_hbm, io_s.at[2])
+    keep.start()
 
     big = [[scatter_ring(chunk(rgp, k, k == 0, w), r_relay.at[k, n], r_main.at[k, n], along(k == 0), 5 * k + n)
             for n, w in enumerate(STEPS)] for k in range(2)]
@@ -501,16 +511,7 @@
     hand_back(1)
     l_back[2].wait_recv()
     l_back[3].wait_recv()
-    zero = jnp.zeros((SL, 128), F32)
-    for g in range(I // 4):
-        sl = slice(g * 128, (g + 1) * 128)
-        tot = lgt[mine, sl].astype(F32) + l_main[0, :, sl].astype(F32) + l_main[1, :, sl].astype(F32)
-        rows4 = jnp.concatenate(
-            [jnp.where(jnp.logical_and(ln128 >= 32 * a, ln128 < 32 * a + 32), tot, zero) for a in range(4)], axis=0)
-        res = dot(rows4.astype(BF16), f4t)
-        for a in range(4):
-            for k in range(2):
-                hg[k, pl.ds(4 * g + a, SL, stride=I), :] = res[a * SL:(a + 1) * SL, k * 128:(k + 1) * 128]
+    ltot_ref[...] = (lgt[mine, :].astype(F32) + l_main[0].astype(F32) + l_main[1].astype(F32)).astype(BF16)
     for k in range(2):
         for t in range(2):
             hop_wait(*back_in(k, t))
@@ -520,25 +521,7 @@
             qp = 4 * m + k
             tq[pl.ds(2 * qp, SL, stride=Q), :] = both
             tq[pl.ds(2 * qp + 1, SL, stride=Q), :] = roll(both, 64)
-    iden_i = eye(I, 128)
-    lni = lanes((I, 128))
-
-    def finish(b, _):
-        rows = 4 * I
-        at = pl.multiple_of(b * rows, rows)
-        tj = dot_nt(iden_i, tq[pl.ds(pl.multiple_of(b * 128, 128), 128), :].astype(BF16))
-        parts = [jnp.where(jnp.logical_and(lni >= 32 * a, lni < 32 * a + 32), tj, 0.0) for a in range(4)]
-        right = dot(jnp.concatenate(parts, axis=0).astype(BF16), g4t)
-        left = jnp.concatenate([hg[0, pl.ds(at, rows), :], hg[1, pl.ds(at, rows), :]], axis=1)
-        grad = (left + right) * scale
-        xn = xhat[pl.ds(at, rows), :]
-        m1 = jnp.mean(grad, axis=-1, keepdims=True)
-        m2 = jnp.mean(grad * xn, axis=-1, keepdims=True)
-        res = (grad - m1 - xn * m2) * rstd[pl.ds(at, rows), :]
-        slope_ref[pl.ds(b * 4, 4)] = res.astype(BF16).reshape(4, I, CH)
-        return 0
-
-    lax.fori_loop(0, SL // 4, finish, 0, unroll=4)
+    tq_ref[...] = tq[...].astype(BF16)
 
     def drain(t, _):
         a2a_copy(t).wait()
@@ -549,27 +532,78 @@
         for copy in ring:
             copy.wait_send()
     own_copy().wait()
+    keep.wait()
     for k in range(2):
         for t in range(2):
             hop_sent(*hop_out(k, t))
             hop_sent(*back_out(k, t))
 
 
+def finish_kernel(out_in, grad_in, x_in, f_ref, g_ref, ltot_in, tq_in, out_ref, grad_ref, slope_ref,
+                  hg, out_v, grad_v, x_ref, ltot_ref, tq_ref, sem):
+    fetch = [pltpu.make_async_copy(src, dst, sem.at[k]) for k, (src, dst) in enumerate(
+        ((ltot_in, ltot_ref), (tq_in, tq_ref), (x_in, x_ref), (out_in, out_v), (grad_in, grad_v)))]
+    for copy in fetch:
+        copy.start()
+    copies = [pltpu.make_async_copy(out_v, out_ref, sem.at[5]), pltpu.make_async_copy(grad_v, grad_ref, sem.at[6])]
+    f4t = dot(tile_rows(), f_ref[...]).astype(BF16)
+    g4t = dot(tile_rows(), g_ref[...]).astype(BF16)
+    ln = lanes((SL, 128))
+    fetch[0].wait()
+    for g in range(I // 4):
+        tot = ltot_ref[:, g * 128:(g + 1) * 128].astype(F32)
+        rows4 = jnp.concatenate(
+            [jnp.where(jnp.logical_and(ln >= 32 * a, ln < 32 * a + 32), tot, 0.0) for a in range(4)], axis=0)
+        res = dot(rows4.astype(BF16), f4t)
+        for a in range(4):
+            for k in range(2):
+                hg[k, pl.ds(4 * g + a, SL, stride=I), :] = res[a * SL:(a + 1) * SL, k * 128:(k + 1) * 128]
+    iden_i = eye(I, 128)
+    lni = lanes((I, 128))
+    for copy in fetch[1:]:
+        copy.wait()
+    for copy in copies:
+        copy.start()
+
+    def finish(b, _):
+        rows = 4 * I
+        at = pl.multiple_of(b * rows, rows)
+        tj = dot_nt(iden_i, tq_ref[pl.ds(pl.multiple_of(b * 128, 128), 128), :])
+        parts = [jnp.where(jnp.logical_and(lni >= 32 * a, lni < 32 * a + 32), tj, 0.0) for a in range(4)]
+        right = dot(jnp.concatenate(parts, axis=0).astype(BF16), g4t)
+        left = jnp.concatenate([hg[0, pl.ds(at, rows), :], hg[1, pl.ds(at, rows), :]], axis=1)
+        grad = (left + right) * (1.0 / S)
+        xn, inv = normalise(x_ref, b)
+        m1 = jnp.mean(grad, axis=-1, keepdims=True)
+        m2 = jnp.mean(grad * xn, axis=-1, keepdims=True)
+        res = (grad - m1 - xn * m2) * inv
+        slope_ref[pl.ds(b * 4, 4)] = res.astype(BF16).reshape(4, I, CH)
+        return 0
+
+    lax.fori_loop(0, SL // 4, finish, 0, unroll=4)
+    for copy in copies:
+        copy.wait()
+
+
 def on_device(profile, pair, loss, former, latter, mixing, expand, shrink):
     vmem = pl.BlockSpec(memory_space=pltpu.VMEM)
     dma = pltpu.SemaphoreType.DMA
-    return pl.pallas_call(
+    anywhere = pl.BlockSpec(memory_space=pl.ANY)
+    ft, gt = former.T, latter.T
+    out, grad, ltot, tq = pl.pallas_call(
         kernel,
         out_shape=(
             jax.ShapeDtypeStruct((IB, J * COLS, C), BF16),
             jax.ShapeDtypeStruct((I, J, C), BF16),
-            jax.ShapeDtypeStruct((SL, I, CH), BF16),
+            jax.ShapeDtypeStruct((SL, I * Q), BF16),
+            jax.ShapeDtypeStruct((SL * Q, 128), BF16),
         ),
-        in_specs=[vmem] * 8,
-        out_specs=(pl.BlockSpec(memory_space=pl.ANY), vmem, vmem),
+        in_specs=[vmem, anywhere, anywhere] + [vmem] * 5,
+        out_specs=(anywhere, anywhere, vmem, vmem),
         scratch_shapes=[
-            pltpu.VMEM((SL * I, CH), F32),
-            pltpu.VMEM((SL * I, 1), F32),
+            pltpu.VMEM((I, J, C), BF16),
+            pltpu.VMEM((I, J, C), BF16),
+            pltpu.VMEM((I, J, C), BF16),
             pltpu.VMEM((SL * I, 128), F32),
             pltpu.VMEM((SL * Q, 128), F32),
             pltpu.VMEM((S, I * Q), BF16),
@@ -590,7 +624,6 @@
             pltpu.VMEM((S, PK), BF16),
             pltpu.VMEM((2, 12, SK, 128), BF16),
             pltpu.VMEM((2, 12, SK, 128), BF16),
-            pltpu.VMEM((2, SL * I, 128), F32),
             pltpu.VMEM((C, I * JP), BF16),
             pltpu.VMEM((C, I * JP), BF16),
             pltpu.VMEM((H, I * JP), BF16),
@@ -600,6 +633,7 @@
             pltpu.VMEM((2, SL, I * Q // 2), BF16),
             pltpu.VMEM((2, SL, I * Q), BF16),
             pltpu.VMEM((4, SL, I * Q), BF16),
+            dma((3,)),
             dma((2, 2)), dma((2, 2)),
             dma((11, 4)), dma((11, 4)),
             dma((8,)), dma((8,)),
@@ -610,7 +644,28 @@
         compiler_params=pltpu.CompilerParams(
             collective_id=0, has_side_effects=True, vmem_limit_bytes=60 * 1024 * 1024),
         cost_estimate=pl.CostEstimate(flops=16_000_000_000, bytes_accessed=8_000_000, transcendentals=3_000_000),
-    )(profile, pair, loss, former.T, latter.T, mixing, expand, shrink)
+    )(profile, pair, loss, ft, gt, mixing, expand, shrink)
+    return pl.pallas_call(
+        finish_kernel,
+        out_shape=(
+            jax.ShapeDtypeStruct((IB, J * COLS, C), BF16),
+            jax.ShapeDtypeStruct((I, J, C), BF16),
+            jax.ShapeDtypeStruct((SL, I, CH), BF16),
+        ),
+        in_specs=[anywhere, anywhere, anywhere, vmem, vmem, anywhere, anywhere],
+        out_specs=(anywhere, anywhere, vmem),
+        scratch_shapes=[
+            pltpu.VMEM((2, SL * I, 128), F32),
+            pltpu.VMEM((IB, J * COLS, C), BF16),
+            pltpu.VMEM((I, J, C), BF16),
+            pltpu.VMEM((SL, I, CH), BF16),
+            pltpu.VMEM((SL, I * Q), BF16),
+            pltpu.VMEM((SL * Q, 128), BF16),
+            dma((7,)),
+        ],
+        compiler_params=pltpu.CompilerParams(vmem_limit_bytes=60 * 1024 * 1024),
+        cost_estimate=pl.CostEstimate(flops=400_000_000, bytes_accessed=6_000_000, transcendentals=2_000),
+    )(out, grad, profile, ft, gt, ltot, tq)
 
 
 def solution(mesh):

time: 90.2 us -> 85 us (0.942)
  local copies, waits for them, and re-layouts: 4.9 us -> 0 us
    pallas_call x1, Pallas kernels: 84.4 us -> 78.7 us  [on_device(): pl.pallas_call(kernel, out_shape=(jax.ShapeDtypeStruct((IB, J * COLS, C),...]
    pallas_call x0 -> x1, Pallas kernels: none -> 5.18 us  [on_device(): pl.pallas_call(finish_kernel, out_shape=(jax.ShapeDtypeStruct((IB, J * CO...]
    unnamed x7 -> x0, local copies, waits for them, and re-layouts: 4.9 us -> none
where the time goes in v5:
time: 85 us; the launch traced here: 84.7 us
  Pallas kernels  83.9 us (99%)
    pallas_call x1, Pallas kernels, on_device(): pl.pallas_call(kernel, out_shape=(jax.ShapeDtypeStruct((IB, J * COLS, C),...  78.7 us
    pallas_call x1, Pallas kernels, on_device(): pl.pallas_call(finish_kernel, out_shape=(jax.ShapeDtypeStruct((IB, J * CO...  5.18 us

profile of v5, /device:TPU:7, one launch (start us, length us, event | category | flops | bytes accessed | tf_op | source)
XLA Modules:
  0.0 84.7 jit_solution(16417387581142647334)
XLA Ops:
  0.6 78.7 %shard_map.103 = (bf16[6,768,128]{2,1,0:T(8,128)(2,1)}, bf16[48,96,128]{2,1,0:T(8,128)(2,1)}, bf16[32,1536]{1,0:T(8,128)(2,1)}, bf16[1024,128]{1,0:T(8,128)(2,1)}) custom-call(bf16[32,48,256]{2,1,0:T(8,128)(2,1)} %x_in.1, bf16[48,96,128]{2,1,0:T(8,128)(2,1)} %pair_hbm.1, bf16[48,96,128]{2,1,0:T(8,128)(2,1)} %loss_hbm.1, bf16[32,256]{1,0:T(8,128)(2,1)} %bitcast.2, ...), custom_call_target="tpu_custom_call" | custom-call | flops 16000000000 | bytes 8000000 | tf_op jit(solution)/shard_map/pallas_call | solution.py:593
  79.4 5.2 %shard_map.104 = (bf16[6,768,128]{2,1,0:T(8,128)(2,1)}, bf16[48,96,128]{2,1,0:T(8,128)(2,1)}, bf16[32,48,256]{2,1,0:T(8,128)(2,1)}) custom-call(bf16[6,768,128]{2,1,0:T(8,128)(2,1)} %get-tuple-element.7.out_in, bf16[48,96,128]{2,1,0:T(8,128)(2,1)} %get-tuple-element.8.grad_in, bf16[32,48,256]{2,1,0:T(8,128)(2,1)} %x_in.1, bf16[32,256]{1,0:T(8,128)(2,1)} %bitcast.3, ...), custom_call_target="tpu_custom_call" | custom-call | flops 400000000 | bytes 6000000 | tf_op jit(solution)/shard_map/pallas_call | solution.py:648

commit v6 on v5

--- a/solution.py
+++ b/solution.py
@@ -238,7 +238,7 @@
         hgs[:, to] = dot(s_ref[...], lob).astype(BF16)
         return 0
 
-    lax.fori_loop(0, 12, ahead, 0, unroll=6)
+    lax.fori_loop(0, 24, ahead, 0, unroll=6)
 
     ln16 = lanes((SK, 128))
     here = pl.ds(pl.multiple_of(r * SK, SK), SK)
@@ -316,13 +316,11 @@
     l_ring[0].start()
     l_ring[1].start()
     l_sibs[0].start()
-    lax.fori_loop(12, 15, ahead, 0, unroll=3)
     for k in range(2):
         for m in range(3):
             first[k][m].wait_recv()
             second[k][1 + m][0].start()
             second[k][1 + m][1].start()
-    lax.fori_loop(15, 18, ahead, 0, unroll=3)
     for m in range(2):
         l_ring[m].wait_recv()
         l_ring[2 + m].start()
@@ -332,7 +330,6 @@
             for m in range(2):
                 second[k][n][m].wait_recv()
                 second[k][n][2 + m].start()
-        lax.fori_loop(18 + 3 * k, 21 + 3 * k, ahead, 0, unroll=3)
     l_ring[2].wait_recv()
     l_ring[3].wait_recv()
     l_sibs[3].start()
@@ -458,8 +455,8 @@
         ring[3].start()
 
     left_grad(0)
-    for n, w in enumerate(STEPS):
-        for k in range(2):
+    for k in range(2):
+        for n, w in enumerate(STEPS):
             relayed(big[k][n], chunk(rgp, k, k == 0, w), r_relay.at[k, n])
     for k in range(1, I * Q // S):
         left_grad(k)

time: 85 us -> 84 us (0.988)
  Pallas kernels: 83.9 us -> 82.9 us
    pallas_call x1, Pallas kernels: 78.7 us -> 77.8 us  [on_device(): pl.pallas_call(kernel, out_shape=(jax.ShapeDtypeStruct((IB, J * COLS, C),...]
where the time goes in v6:
time: 84 us; the launch traced here: 83.7 us
  Pallas kernels  82.9 us (99%)
    pallas_call x1, Pallas kernels, on_device(): pl.pallas_call(kernel, out_shape=(jax.ShapeDtypeStruct((IB, J * COLS, C),...  77.8 us
    pallas_call x1, Pallas kernels, on_device(): pl.pallas_call(finish_kernel, out_shape=(jax.ShapeDtypeStruct((IB, J * CO...  5.18 us

profile of v6, /device:TPU:7, one launch (start us, length us, event | category | flops | bytes accessed | tf_op | source)
XLA Modules:
  0.0 83.7 jit_solution(9546398951984924120)
XLA Ops:
  0.6 77.8 %shard_map.103 = (bf16[6,768,128]{2,1,0:T(8,128)(2,1)}, bf16[48,96,128]{2,1,0:T(8,128)(2,1)}, bf16[32,1536]{1,0:T(8,128)(2,1)}, bf16[1024,128]{1,0:T(8,128)(2,1)}) custom-call(bf16[32,48,256]{2,1,0:T(8,128)(2,1)} %x_in.1, bf16[48,96,128]{2,1,0:T(8,128)(2,1)} %pair_hbm.1, bf16[48,96,128]{2,1,0:T(8,128)(2,1)} %loss_hbm.1, bf16[32,256]{1,0:T(8,128)(2,1)} %bitcast.2, ...), custom_call_target="tpu_custom_call" | custom-call | flops 16000000000 | bytes 8000000 | tf_op jit(solution)/shard_map/pallas_call | solution.py:590
  78.4 5.2 %shard_map.104 = (bf16[6,768,128]{2,1,0:T(8,128)(2,1)}, bf16[48,96,128]{2,1,0:T(8,128)(2,1)}, bf16[32,48,256]{2,1,0:T(8,128)(2,1)}) custom-call(bf16[6,768,128]{2,1,0:T(8,128)(2,1)} %get-tuple-element.7.out_in, bf16[48,96,128]{2,1,0:T(8,128)(2,1)} %get-tuple-element.8.grad_in, bf16[32,48,256]{2,1,0:T(8,128)(2,1)} %x_in.1, bf16[32,256]{1,0:T(8,128)(2,1)} %bitcast.3, ...), custom_call_target="tpu_custom_call" | custom-call | flops 400000000 | bytes 6000000 | tf_op jit(solution)/shard_map/pallas_call | solution.py:645
